TPU v7x, 32 devices: a whole 2x2x4 slice. The times are simulated.
32 devices in a mesh: parts: 2 (over x), seq: 16 (over z, y, core).
Axes of the slice: x: 2, y: 2, z: 4, core: 2. Of those that a mesh axis runs over, the one named last changes fastest.
Arguments:
- latent: float32 [3072, 64], P(('parts', 'seq')), parts along dimension 0, may hold values from -6 to 6
- main_hidden: bfloat16 [3072, 5120], P(('parts', 'seq')), parts along dimension 0, may hold values from -10 to 10
- main_query: bfloat16 [3072, 5120], P(('parts', 'seq')), parts along dimension 0, may hold values from -40 to 40
- text_key: bfloat16 [1024, 5120], P(('parts', 'seq')), parts along dimension 0, may hold values from -40 to 40
- text_value: bfloat16 [1024, 5120], P(('parts', 'seq')), parts along dimension 0, may hold values from -12 to 12
- text_len: int32 [2], P('parts'), parts along dimension 0, may hold values from 128 to 512
- guide_hidden: bfloat16 [3072, 1536], P(('parts', 'seq')), parts along dimension 0, may hold values from -10 to 10
- guide_query: bfloat16 [3072, 768], P(('parts', 'seq')), parts along dimension 0, may hold values from -40 to 40
- guide_key: bfloat16 [3072, 768], P(('parts', 'seq')), parts along dimension 0, may hold values from -40 to 40
- guide_value: bfloat16 [3072, 768], P(('parts', 'seq')), parts along dimension 0, may hold values from -48 to 48
- guide_out: bfloat16 [768, 1536], replicated, may hold values from -0.21875 to 0.21875
- main_head: bfloat16 [5120, 64], replicated, may hold values from -0.078125 to 0.078125
- guide_head: bfloat16 [1536, 64], replicated, may hold values from -0.15625 to 0.15625
- main_modulation: float32 [4, 5120], P('parts'), parts along dimension 0, may hold values from -1.5 to 1.5
- guide_modulation: float32 [4, 1536], P('parts'), parts along dimension 0, may hold values from -1.5 to 1.5
- guidance_scale: float32 [2], P('parts'), parts along dimension 0, may hold values from 1.5 to 3.5
- sigma_table: float32 [51], replicated, may hold values from 0 to 1, as said below
- step_index: int32 [2], P('parts'), parts along dimension 0, may hold values from 0 to 49
Outputs:
- velocity: float32 [3072, 64], P(('parts', 'seq')), parts along dimension 0
- next_latent: float32 [3072, 64], P(('parts', 'seq')), parts along dimension 0
There are 2 independent parts, one for each index of `parts`. A program takes and returns all parts, laid end to end along the dimension named above; an argument that names none is the same for every part. Nothing has to cross between parts.
Inputs may be any that keep to these rules, and one draw needn't show every extreme that they name: `sigma_table`: falls from 1 at index 0 to a small positive value at index 50.
All inputs are finite; a program needn't handle non-finite values.
Results may differ from a plain program's by a relative error of at most 0.0055.
Values may be sent and summed in bfloat16 or wider, within the bound.
A program may use at most 192 MiB of HBM per device.

v0:
```python
import jax
import jax.numpy as jnp
from jax import lax
from jax.sharding import PartitionSpec as P

HDIM = 128


def start_state(height, heads, head_size):
    return (
        jnp.full((heads, height), -1e30, jnp.float32),
        jnp.zeros((heads, height), jnp.float32),
        jnp.zeros((heads, height, head_size), jnp.float32),
    )


def fold_step(running, queries, keys, values, heads, valid):
    height = queries.shape[0]
    head_size = queries.shape[1] // heads
    query_heads = queries.reshape(height, heads, head_size)
    key_heads = keys.reshape(keys.shape[0], heads, head_size)
    value_heads = values.reshape(values.shape[0], heads, head_size)
    scores = jnp.einsum(
        "qhd,khd->hqk", query_heads, key_heads, preferred_element_type=jnp.float32
    ) * head_size ** (-0.5)
    if valid is not None:
        scores = jnp.where(valid[None, None, :], scores, -1e30)
    peak_old, totals, accumulated = running
    peak_new = jnp.maximum(peak_old, jnp.max(scores, axis=-1))
    weights = jnp.exp(scores - peak_new[..., None])
    if valid is not None:
        weights = jnp.where(valid[None, None, :], weights, 0.0)
    totals = jnp.sum(weights, axis=-1)
    accumulated = jnp.einsum(
        "hqk,khd->hqd",
        weights.astype(jnp.bfloat16),
        value_heads,
        preferred_element_type=jnp.float32,
    )
    return (peak_new, totals, accumulated)


def finish(running):
    peak, totals, accumulated = running
    result = accumulated / totals[..., None]
    return result.transpose(1, 0, 2).reshape(result.shape[1], -1).astype(jnp.bfloat16)


def head_out(summed, modulation, head_weight):
    centered = summed - jnp.mean(summed, axis=-1, keepdims=True)
    spread = jnp.mean(centered * centered, axis=-1, keepdims=True)
    normed = centered * lax.rsqrt(spread + 1e-06)
    shaped = (normed * (1.0 + modulation[1]) + modulation[0]).astype(jnp.bfloat16)
    return jnp.dot(shaped, head_weight, preferred_element_type=jnp.float32)


def per_device(
    latent,
    main_hidden,
    main_query,
    text_key,
    text_value,
    text_len,
    guide_hidden,
    guide_query,
    guide_key,
    guide_value,
    guide_out,
    main_head,
    guide_head,
    main_modulation,
    guide_modulation,
    guidance_scale,
    sigma_table,
    step_index,
):
    height = main_query.shape[0]
    main_heads = main_head.shape[0] // HDIM
    guide_heads = guide_out.shape[0] // HDIM
    all_text_keys = lax.all_gather(text_key, "seq", axis=0, tiled=True)
    all_text_values = lax.all_gather(text_value, "seq", axis=0, tiled=True)
    positions = jnp.arange(all_text_keys.shape[0], dtype=jnp.int32)
    folded = fold_step(
        start_state(height, main_heads, HDIM),
        main_query,
        all_text_keys,
        all_text_values,
        main_heads,
        positions < text_len[0],
    )
    main_sum = main_hidden.astype(jnp.float32) + finish(folded).astype(jnp.float32)
    main_velocity = head_out(main_sum, main_modulation, main_head)
    all_keys = lax.all_gather(guide_key, "seq", axis=0, tiled=True)
    all_values = lax.all_gather(guide_value, "seq", axis=0, tiled=True)
    folded = fold_step(
        start_state(height, guide_heads, HDIM), guide_query, all_keys, all_values, guide_heads, None
    )
    projected = jnp.dot(finish(folded), guide_out, preferred_element_type=jnp.float32)
    guide_sum = guide_hidden.astype(jnp.float32) + projected
    guide_velocity = head_out(guide_sum, guide_modulation, guide_head)
    velocity = guide_velocity + guidance_scale[0] * (main_velocity - guide_velocity)
    positions = jnp.arange(sigma_table.shape[0], dtype=jnp.int32)
    sigma_now = jnp.sum(jnp.where(positions == step_index[0], sigma_table, 0.0))
    sigma_next = jnp.sum(jnp.where(positions == step_index[0] + 1, sigma_table, 0.0))
    next_latent = latent + (sigma_next - sigma_now) * velocity
    return (velocity, next_latent)


def solution(mesh):
    placed = (
        P(("parts", "seq"), None),
        P(("parts", "seq"), None),
        P(("parts", "seq"), None),
        P(("parts", "seq"), None),
        P(("parts", "seq"), None),
        P("parts"),
        P(("parts", "seq"), None),
        P(("parts", "seq"), None),
        P(("parts", "seq"), None),
        P(("parts", "seq"), None),
        P(),
        P(),
        P(),
        P("parts", None),
        P("parts", None),
        P("parts"),
        P(),
        P("parts"),
    )
    return jax.shard_map(
        per_device,
        mesh=mesh,
        in_specs=placed,
        out_specs=(P(("parts", "seq"), None), P(("parts", "seq"), None)),
        check_vma=False,
    )
```

profile of v0, /device:TPU:0, one launch (start us, length us, event | category | flops | bytes accessed | tf_op | source)
XLA Modules:
  0.0 235.6 jit_solution(11607706279006849806)
XLA Ops:
  7.2 0.0 copy-start
  7.2 0.0 all-gather.5.cloned.1.call-start
  7.2 0.7 all-gather.5.cloned.1.call-update
  7.9 0.0 all-gather.7.cloned.1.call-start
  8.0 0.7 all-gather.7.cloned.1.call-update
  8.7 0.0 all-gather.9.cloned.1.call-start
  8.7 0.7 all-gather.9.cloned.1.call-update
  9.4 0.0 all-gather.11.cloned.1.call-start
  9.4 0.5 all-gather.11.cloned.1.call-update
  11.9 1.3 fusion.51
  14.5 0.8 add_reduce_fusion
  15.3 0.9 slice_add_fusion
  16.2 39.0 %all-gather.5.cloned.1.call-done = bf16[1536,768]{1,0:T(8,128)(2,1)} async-done(((bf16[96,768]{1,0:T(8,128)(2,1)}), bf16[1536,768]{1,0:T(8,128)(2,1)}) %all-gather.5.cloned.1.call-update) | async-done | bytes 2359312 | tf_op jit(solution)/shard_map/all_gather | solution.py:93
  55.2 4.3 %copy.34 = bf16[1536,768]{0,1:T(8,128)(2,1)} copy(bf16[1536,768]{1,0:T(8,128)(2,1)} %all-gather.5.cloned.1.call-done) | data formatting | bytes 4718592 | tf_op jit(solution)/shard_map/all_gather | solution.py:93
  59.5 0.0 copy-start.6
  59.5 39.0 %all-gather.7.cloned.1.call-done = bf16[1536,768]{1,0:T(8,128)(2,1)} async-done(((bf16[96,768]{1,0:T(8,128)(2,1)}), bf16[1536,768]{1,0:T(8,128)(2,1)}) %all-gather.7.cloned.1.call-update) | async-done | bytes 2359312 | tf_op jit(solution)/shard_map/all_gather | solution.py:94
  98.6 4.3 %copy.37 = bf16[1536,768]{0,1:T(8,128)(2,1)} copy(bf16[1536,768]{1,0:T(8,128)(2,1)} %all-gather.7.cloned.1.call-done) | data formatting | bytes 4718592 | tf_op jit(solution)/shard_map/all_gather | solution.py:94
  102.8 0.0 copy-done.6
  102.8 0.0 copy-start.2
  102.8 2.5 %fusion.55 = (f32[6,96]{1,0:T(8,128)S(1)}, f32[6,96,1536]{2,1,0:T(8,128)S(1)}) fusion(bf16[1536,6,128]{0,2,1:T(8,128)(2,1)} %bitcast.76, bf16[96,768]{1,0:T(8,128)(2,1)S(1)} %copy-done.6), kind=kOutput, calls=%fused_computation.67 | convolution fusion | flops 228261312 | bytes 6048000 | tf_op jit(solution)/shard_map/qhd,khd->hqk/dot_general | solution.py:23
  105.4 0.6 fusion.10
  106.0 0.0 copy-start.5
  106.0 0.0 copy-done.2
  106.0 0.0 copy-start.8
  106.0 0.9 fusion.29
  107.0 0.0 copy-done
  107.0 0.0 copy-done.5
  107.0 0.6 fusion.56
  107.6 0.2 multiply_reduce_fusion.1
  107.9 0.0 copy-done.8
  107.9 0.3 fusion.41
  108.2 0.0 copy-start.4
  108.2 47.5 %all-gather.9.cloned.1.call-done = bf16[512,5120]{1,0:T(8,128)(2,1)} async-done(((bf16[32,5120]{1,0:T(8,128)(2,1)}), bf16[512,5120]{1,0:T(8,128)(2,1)}) %all-gather.9.cloned.1.call-update) | async-done | bytes 5242896 | tf_op jit(solution)/shard_map/all_gather | solution.py:80
  155.7 7.9 %copy.40 = bf16[512,5120]{0,1:T(8,128)(2,1)} copy(bf16[512,5120]{1,0:T(8,128)(2,1)} %all-gather.9.cloned.1.call-done) | data formatting | bytes 10485760 | tf_op jit(solution)/shard_map/all_gather | solution.py:80
  163.7 0.0 copy-done.4
  163.7 4.2 %fusion = (f32[40,96]{1,0:T(8,128)S(1)}, f32[40,96,512]{2,1,0:T(8,128)S(1)}) fusion(pred[512]{0:T(512)(128)(4,1)S(1)} %iota_compare_fusion, bf16[512,40,128]{0,2,1:T(8,128)(2,1)} %bitcast.74, bf16[96,5120]{1,0:T(8,128)(2,1)S(1)} %copy-done.4), kind=kOutput, calls=%fused_computation.2 | convolution fusion | flops 509210880 | bytes 14106112 | tf_op jit(solution)/shard_map/qhd,khd->hqk/dot_general | solution.py:23
  167.8 0.0 copy-start.1
  167.8 3.1 %copy-done.1 = f32[40,96,512]{2,1,0:T(8,128)} copy-done((f32[40,96,512]{2,1,0:T(8,128)}, f32[40,96,512]{2,1,0:T(8,128)S(1)}, u32[]{:S(2)}) %copy-start.1) | copy-done | bytes 7864344
  170.9 2.4 %fusion.1 = f32[40,96]{1,0:T(8,128)S(1)} fusion(f32[40,96,512]{2,1,0:T(8,128)S(1)} %get-tuple-element.13, f32[40,96]{1,0:T(8,128)S(1)} %broadcast_maximum_fusion, pred[512]{0:T(512)(128)(4,1)S(1)} %iota_compare_fusion), kind=kLoop, calls=%fused_computation.3 | loop fusion | flops 9826560 | bytes 7895552 | tf_op jit(solution)/shard_map/reduce_sum | solution.py:33
  173.4 39.1 %all-gather.11.cloned.1.call-done = bf16[512,5120]{1,0:T(8,128)(2,1)} async-done(((bf16[32,5120]{1,0:T(8,128)(2,1)}), bf16[512,5120]{1,0:T(8,128)(2,1)}) %all-gather.11.cloned.1.call-update) | async-done | bytes 5242896 | tf_op jit(solution)/shard_map/all_gather | solution.py:81
  212.4 7.9 %copy.43 = bf16[512,5120]{0,1:T(8,128)(2,1)} copy(bf16[512,5120]{1,0:T(8,128)(2,1)} %all-gather.11.cloned.1.call-done) | data formatting | bytes 10485760 | tf_op jit(solution)/shard_map/all_gather | solution.py:81
  220.4 0.0 copy-start.3
  220.4 6.3 %convert_bitcast_fusion = f32[40,12,8,128]{3,2,1,0:T(8,128)S(1)} fusion(bf16[512,40,128]{0,2,1:T(8,128)(2,1)} %bitcast.77, f32[40,96,512]{2,1,0:T(8,128)} %copy-done.1, f32[40,96]{1,0:T(8,128)S(1)} %broadcast_maximum_fusion, pred[512]{0:T(512)(128)(4,1)S(1)} %iota_compare_fusion, f32[96,40]{0,1:T(8,128)S(1)} %bitcast.78), kind=kOutput, calls=%fused_computation.19 | convolution fusion | flops 514621440 | bytes 15104512 | tf_op jit(solution)/shard_map/hqk,khd->hqd/dot_general | solution.py:34
  226.7 0.0 copy-done.3
  226.7 0.0 copy-start.7
  226.8 0.0 copy-start.9
  226.8 0.3 fusion.40
  227.1 0.5 multiply_reduce_fusion
  227.6 0.3 copy-done.7
  227.8 0.0 copy-done.9
  227.8 1.3 multiply_add_fusion
  (7 shorter events, 0.0 us)
Async XLA Ops:
  7.2 99.8 %copy-start = (bf16[768,1536]{1,0:T(8,128)(2,1)S(1)}, bf16[768,1536]{1,0:T(8,128)(2,1)}, u32[]{:S(2)}) copy-start(bf16[768,1536]{1,0:T(8,128)(2,1)} %param.28) | copy-start | bytes 7077892
  7.2 48.1 %all-gather.5.cloned.1.call-start = ((), (), s32[]{:S(2)}) async-start(), calls=%async_computation | async-start | bytes 2506752 | tf_op jit(solution)/shard_map/all_gather | solution.py:93
  7.9 90.6 %all-gather.7.cloned.1.call-start = ((), (), s32[]{:S(2)}) async-start(), calls=%async_computation.1 | async-start | bytes 2506752 | tf_op jit(solution)/shard_map/all_gather | solution.py:94
  8.7 147.0 %all-gather.9.cloned.1.call-start = ((), (), s32[]{:S(2)}) async-start(), calls=%async_computation.2 | async-start | bytes 5570560 | tf_op jit(solution)/shard_map/all_gather | solution.py:80
  9.4 203.0 %all-gather.11.cloned.1.call-start = ((), (), s32[]{:S(2)}) async-start(), calls=%async_computation.3 | async-start | bytes 5570560 | tf_op jit(solution)/shard_map/all_gather | solution.py:81
  59.5 43.3 %copy-start.6 = (bf16[96,768]{1,0:T(8,128)(2,1)S(1)}, bf16[96,768]{1,0:T(8,128)(2,1)}, u32[]{:S(2)}) copy-start(bf16[96,768]{1,0:T(8,128)(2,1)} %param.25) | copy-start | bytes 442372
  102.8 3.2 %copy-start.2 = (bf16[1536,768]{0,1:T(8,128)(2,1)S(1)}, bf16[1536,768]{0,1:T(8,128)(2,1)}, u32[]{:S(2)}) copy-start(bf16[1536,768]{0,1:T(8,128)(2,1)} %copy.37) | copy-start | bytes 7077892
  106.0 1.0 copy-start.5
  106.0 1.8 copy-start.8
  108.2 55.5 %copy-start.4 = (bf16[96,5120]{1,0:T(8,128)(2,1)S(1)}, bf16[96,5120]{1,0:T(8,128)(2,1)}, u32[]{:S(2)}) copy-start(bf16[96,5120]{1,0:T(8,128)(2,1)} %param.20) | copy-start | bytes 2949124
  167.8 3.1 %copy-start.1 = (f32[40,96,512]{2,1,0:T(8,128)}, f32[40,96,512]{2,1,0:T(8,128)S(1)}, u32[]{:S(2)}) copy-start(f32[40,96,512]{2,1,0:T(8,128)S(1)} %get-tuple-element.13) | copy-start | bytes 23592964
  220.4 6.3 %copy-start.3 = (bf16[96,5120]{1,0:T(8,128)(2,1)S(1)}, bf16[96,5120]{1,0:T(8,128)(2,1)}, u32[]{:S(2)}) copy-start(bf16[96,5120]{1,0:T(8,128)(2,1)} %param.19) | copy-start | bytes 2949124
  226.7 1.1 copy-start.7
  226.8 1.1 copy-start.9
Sparse Core Ops, SparseCore 0:
  10.3 44.9 all-gather.4
  57.5 40.9 all-gather.6
  100.8 54.8 all-gather.8
  157.8 54.5 all-gather.10
where the time goes:
time: 236 us
  waiting for transfers between devices  167 us (71%)
  local copies, waits for them, and re-layouts  27.9 us (12%)
  between operations  17.1 us (7%)
  matrix products  16.1 us (7%)
  other arithmetic  7.15 us (3%)
    all_gather x1, waiting for transfers between devices, per_device(): all_text_keys = lax.all_gather(text_key, 'seq', axis=0, tiled=True)  47.5 us
    all_gather x1, waiting for transfers between devices, per_device(): all_text_values = lax.all_gather(text_value, 'seq', axis=0, tiled=True)  39.1 us
    all_gather x1, waiting for transfers between devices, per_device(): all_values = lax.all_gather(guide_value, 'seq', axis=0, tiled=True)  39 us
    all_gather x1, waiting for transfers between devices, per_device(): all_keys = lax.all_gather(guide_key, 'seq', axis=0, tiled=True)  39 us
    all_gather x1, local copies, waits for them, and re-layouts, per_device(): all_text_keys = lax.all_gather(text_key, 'seq', axis=0, tiled=True)  7.95 us
    all_gather x1, local copies, waits for them, and re-layouts, per_device(): all_text_values = lax.all_gather(text_value, 'seq', axis=0, tiled=True)  7.95 us
    dot_general x2, matrix products, fold_step(): jnp.einsum('hqk,khd->hqd', weights.astype(jnp.bfloat16), value_heads, pre...  7.28 us
    dot_general x2, matrix products, fold_step(): jnp.einsum('qhd,khd->hqk', query_heads, key_heads, preferred_element_type...  6.68 us
  transfers between devices with their start and end apart: 4, of which 4 were waited for; matrix products, arithmetic and copies ran while one was open for 13% of the time, Pallas kernels for 0%

commit v1 on v0

--- a/solution.py
+++ b/solution.py
@@ -1,6 +1,11 @@
+import functools
+import math
+
 import jax
 import jax.numpy as jnp
 from jax import lax
+from jax.experimental import pallas as pl
+from jax.experimental.pallas import tpu as pltpu
 from jax.sharding import PartitionSpec as P
 
 HDIM = 128
@@ -106,6 +111,621 @@
     return (velocity, next_latent)
 
 
+def layout(mesh):
+    axis = mesh.axis_names.index("seq")
+    devices = mesh.devices
+    for other in range(devices.ndim - 1, -1, -1):
+        if other != axis:
+            devices = devices.take(0, axis=other)
+    places = [getattr(device, "coords", None) for device in devices]
+    if places[0] is None:
+        return 1, 1
+    slab = sum(place[2] == places[0][2] for place in places)
+    cores = sum(tuple(place) == tuple(places[0]) for place in places)
+    return slab, cores
+
+
+def shaped_rows(summed, modulation):
+    centered = summed - jnp.mean(summed, axis=-1, keepdims=True)
+    spread = jnp.mean(centered * centered, axis=-1, keepdims=True)
+    normed = centered * lax.rsqrt(spread + 1e-06)
+    return (normed * (1.0 + modulation[1:2]) + modulation[0:1]).astype(jnp.bfloat16)
+
+
+def kernel(
+    slabs,
+    slab,
+    cores,
+    text_len,
+    guidance_scale,
+    sigma_table,
+    step_index,
+    latent,
+    main_hidden,
+    main_query,
+    text_key,
+    text_value,
+    guide_hidden,
+    guide_query,
+    guide_key,
+    guide_value,
+    guide_out,
+    main_head,
+    guide_head,
+    main_modulation,
+    guide_modulation,
+    velocity,
+    next_latent,
+    tk,
+    tv,
+    tq,
+    to,
+    att,
+    gk,
+    gv,
+    gq,
+    gacc,
+    gml,
+    racc,
+    rml,
+    v_latent,
+    v_hidden,
+    v_ghidden,
+    v_gout,
+    v_mhead,
+    v_ghead,
+    v_mmod,
+    v_gmod,
+    v_shaped,
+    v_gshaped,
+    local_sem,
+    load_sem,
+    t_send,
+    t_recv,
+    q_send,
+    q_recv,
+    g_send,
+    g_recv,
+    own_send,
+    near_recv,
+    fwd_send,
+    far_recv,
+    gc_send,
+    gc_recv,
+    o_send,
+    o_recv,
+    p_send,
+    p_recv,
+):
+    me = lax.axis_index("seq")
+    z = me // slab
+    s = me % slab
+    c = s % cores
+    rows = main_query.shape[0]
+    text_cols = tk.shape[-1]
+    guide_cols = gk.shape[-1]
+    heads = text_cols // HDIM
+    guide_heads = guide_cols // HDIM
+    keys = slabs * slab * tk.shape[2]
+    guide_keys = slabs * cores * rows
+    scale = HDIM ** (-0.5) * math.log2(math.e)
+
+    def cols(ref, index, width):
+        return ref.at[:, pl.ds(pl.multiple_of(index * width, 128), width)]
+
+    def remote(src, dst, send, recv, target):
+        return pltpu.make_async_remote_copy(
+            src_ref=src,
+            dst_ref=dst,
+            send_sem=send,
+            recv_sem=recv,
+            device_id={"seq": target},
+            device_id_type=pl.DeviceIdType.MESH,
+        )
+
+    def peer(j):
+        return (s - c + (j // cores) * cores) % slab + (c + j) % cores
+
+    def back(j):
+        return (slab // cores - j // cores) % (slab // cores) * cores + (cores - j) % cores
+
+    mine = [
+        (cols(text_key, s, text_cols), tk.at[z, s]),
+        (cols(text_value, s, text_cols), tv.at[z, s]),
+        (cols(main_query, s, text_cols), tq.at[s]),
+        (cols(guide_query, c, guide_cols), gq.at[s]),
+        (cols(guide_key, c, guide_cols), gk.at[z, c]),
+        (cols(guide_value, c, guide_cols), gv.at[z, c]),
+    ]
+    mine = [pltpu.make_async_copy(a, b, local_sem.at[i]) for i, (a, b) in enumerate(mine)]
+    loads = [
+        (main_hidden, v_hidden),
+        (main_head, v_mhead),
+        (main_modulation, v_mmod),
+        (guide_out, v_gout),
+        (guide_hidden, v_ghidden),
+        (guide_head, v_ghead),
+        (guide_modulation, v_gmod),
+        (latent, v_latent),
+    ]
+    loads = [pltpu.make_async_copy(a, b, load_sem.at[i]) for i, (a, b) in enumerate(loads)]
+    for copy in mine:
+        copy.start()
+
+    barrier = pltpu.get_barrier_semaphore()
+
+    def greet(target):
+        pl.semaphore_signal(
+            barrier, inc=1, device_id={"seq": target}, device_id_type=pl.DeviceIdType.MESH
+        )
+
+    for j in range(1, slab):
+        greet(z * slab + peer(j))
+
+    @pl.when(z > 0)
+    def _():
+        greet(me - slab)
+
+    @pl.when(z < slabs - 1)
+    def _():
+        greet(me + slab)
+
+    ends = jnp.where(z > 0, 1, 0) + jnp.where(z < slabs - 1, 1, 0)
+    pl.semaphore_wait(barrier, slab - 1 + ends)
+
+    target = (me - slab, me + slab)
+    has_target = (z > 0, z < slabs - 1)
+    sent = []
+
+    def both_ways(make):
+        for way in range(2):
+
+            @pl.when(has_target[way])
+            def _(way=way):
+                for copy in make(way):
+                    copy.start()
+
+            sent.append((has_target[way], functools.partial(make, way)))
+
+    both = ((text_key, tk), (text_value, tv))
+    guide_both = ((guide_key, gk), (guide_value, gv))
+
+    def slab_text(j, kv):
+        source, place = both[kv]
+        t = peer(j)
+        return remote(
+            cols(source, t, text_cols),
+            place.at[z, s],
+            t_send.at[j, kv],
+            t_recv.at[back(j), kv],
+            z * slab + t,
+        )
+
+    def chain_own(j, kv, way):
+        source, place = both[kv]
+        t = peer(j)
+        src = cols(source, s, text_cols) if j == 0 else place.at[z, t]
+        return remote(
+            src, place.at[z, t], own_send.at[way, j, kv], near_recv.at[way, j, kv], target[way]
+        )
+
+    def slab_guide(j, kv):
+        source, place = guide_both[kv]
+        t = peer(j)
+        return remote(
+            cols(source, t % cores, guide_cols),
+            place.at[z, c],
+            g_send.at[j, kv],
+            g_recv.at[back(j), kv],
+            z * slab + t,
+        )
+
+    def slab_query(j):
+        t = peer(j)
+        return (
+            remote(
+                cols(main_query, t, text_cols),
+                tq.at[s],
+                q_send.at[j, 0],
+                q_recv.at[back(j), 0],
+                z * slab + t,
+            ),
+            remote(
+                cols(guide_query, t % cores, guide_cols),
+                gq.at[s],
+                q_send.at[j, 1],
+                q_recv.at[back(j), 1],
+                z * slab + t,
+            ),
+        )
+
+    for kv in range(2):
+        for j in range(slab - 1, 0, -1):
+            slab_text(j, kv).start()
+        both_ways(lambda way, kv=kv: [chain_own(0, kv, way)])
+    for kv in range(2):
+        for j in range(1, cores):
+            slab_guide(j, kv).start()
+    for j in range(slab - 1, 0, -1):
+        for copy in slab_query(j):
+            copy.start()
+    for copy in loads:
+        copy.start()
+
+    def arrived(place, sem):
+        pltpu.make_async_copy(place, place, sem).wait()
+
+    for kv in range(2):
+        place = both[kv][1]
+        for j in range(1, slab):
+            arrived(place.at[z, peer(j)], t_recv.at[j, kv])
+            both_ways(lambda way, kv=kv, j=j: [chain_own(j, kv, way)])
+    for copy in mine:
+        copy.wait()
+    for kv in range(2):
+        place = guide_both[kv][1]
+        for j in range(1, cores):
+            arrived(place.at[z, peer(j) % cores], g_recv.at[j, kv])
+
+    def guide_chain(d, kv, way):
+        place = guide_both[kv][1]
+        from_z = z + d if way == 0 else z - d
+        return remote(
+            place.at[from_z],
+            place.at[from_z],
+            gc_send.at[way, d, kv],
+            gc_recv.at[way, d, kv],
+            target[way],
+        )
+
+    both_ways(lambda way: [guide_chain(0, 0, way), guide_chain(0, 1, way)])
+
+    def text_chain(d, kv, way):
+        place = both[kv][1]
+        from_z = z + d if way == 0 else z - d
+        return remote(
+            place.at[from_z],
+            place.at[from_z],
+            fwd_send.at[way, d, kv],
+            far_recv.at[way, d, kv],
+            target[way],
+        )
+
+    for d in range(1, slabs):
+        for kv in range(2):
+            place = both[kv][1]
+            for way in range(2):
+                from_z = z + d if way == 0 else z - d
+                comes = from_z < slabs if way == 0 else from_z >= 0
+
+                @pl.when(comes)
+                def _(way=way, kv=kv, d=d, place=place, from_z=from_z):
+                    if d == 1:
+                        for j in range(slab):
+                            arrived(place.at[from_z, peer(j)], near_recv.at[way, j, kv])
+                    else:
+                        arrived(place.at[from_z], far_recv.at[way, d - 1, kv])
+
+                if d < slabs - 1:
+                    goes = jnp.logical_and(comes, has_target[way])
+
+                    @pl.when(goes)
+                    def _(way=way, kv=kv, d=d):
+                        text_chain(d, kv, way).start()
+
+                    sent.append((goes, lambda way=way, kv=kv, d=d: [text_chain(d, kv, way)]))
+
+    def guide_arrived(d, way):
+        from_z = z + d if way == 0 else z - d
+        for kv in range(2):
+            arrived(guide_both[kv][1].at[from_z], gc_recv.at[way, d - 1, kv])
+
+    for d in range(1, slabs):
+        for way in range(2):
+            comes = z + d < slabs if way == 0 else z - d >= 0
+            goes = jnp.logical_and(comes, has_target[way])
+
+            @pl.when(goes)
+            def _(way=way, d=d):
+                guide_arrived(d, way)
+                if d < slabs - 1:
+                    for kv in range(2):
+                        guide_chain(d, kv, way).start()
+
+            if d < slabs - 1:
+                sent.append(
+                    (goes, lambda way=way, d=d: [guide_chain(d, kv, way) for kv in range(2)])
+                )
+
+    for j in range(1, slab):
+        arrived(tq.at[peer(j)], q_recv.at[j, 0])
+        arrived(gq.at[peer(j)], q_recv.at[j, 1])
+
+    positions = lax.broadcasted_iota(jnp.int32, (1, keys), 1)
+    bias = jnp.where(positions < text_len[0], 0.0, -1e30).astype(jnp.float32)
+
+    def weigh(q, k, bias=None):
+        scores = lax.dot_general(
+            q, k, (((1,), (1,)), ((), ())), preferred_element_type=jnp.float32
+        )
+        if bias is not None:
+            scores = scores + bias
+        peak = jnp.max(scores, axis=-1, keepdims=True)
+        weights = jnp.exp2((scores - peak) * scale)
+        return peak, weights, jnp.sum(weights, axis=-1, keepdims=True)
+
+    groups = 2 if heads % 2 == 0 else 1
+    width = text_cols // groups
+
+    def give(j, group):
+        t = peer(j)
+        at = pl.ds(pl.multiple_of(s * text_cols + group * width, 128), width)
+        return remote(
+            to.at[t, :, pl.ds(group * width, width)],
+            att.at[:, at],
+            o_send.at[j, group],
+            o_recv.at[back(j), group],
+            z * slab + t,
+        )
+
+    for group in range(groups):
+
+        def one_head(h, _):
+            at = pl.ds(pl.multiple_of(group * width + h * HDIM, 128), HDIM)
+            k = tk[:, :, :, at].reshape(keys, HDIM)
+            v = tv[:, :, :, at].reshape(keys, HDIM)
+            for t in range(slab):
+                _, weights, total = weigh(tq[t, :, at], k, bias)
+                out = jnp.dot(weights.astype(jnp.bfloat16), v, preferred_element_type=jnp.float32)
+                to[t, :, at] = (out / total).astype(jnp.bfloat16)
+            return 0
+
+        lax.fori_loop(0, heads // groups, one_head, 0)
+        for j in range(slab - 1, 0, -1):
+            give(j, group).start()
+    own_att = pltpu.make_async_copy(to.at[s], cols(att, s, text_cols), local_sem.at[0])
+    own_att.start()
+
+    for d in range(1, slabs):
+        for way in range(2):
+            comes = z + d < slabs if way == 0 else z - d >= 0
+            last = jnp.logical_and(comes, jnp.logical_not(has_target[way]))
+
+            @pl.when(last)
+            def _(way=way, d=d):
+                guide_arrived(d, way)
+
+    for h in range(guide_heads):
+        at = pl.ds(h * HDIM, HDIM)
+
+        def one_owner(t, _):
+            k = gk[:, :, :, at].reshape(guide_keys, HDIM)
+            v = gv[:, :, :, at].reshape(guide_keys, HDIM)
+            peak, weights, total = weigh(gq[t, :, at], k)
+            gacc[t, :, at] = jnp.dot(
+                weights.astype(jnp.bfloat16), v, preferred_element_type=jnp.float32
+            )
+            gml[t, :, h : h + 1] = peak
+            gml[t, :, guide_heads + h : guide_heads + h + 1] = total
+            return 0
+
+        lax.fori_loop(0, slab, one_owner, 0)
+
+    def part(j):
+        t = peer(j)
+        return (
+            remote(gacc.at[t], racc.at[s], p_send.at[j, 0], p_recv.at[back(j), 0], z * slab + t),
+            remote(gml.at[t], rml.at[s], p_send.at[j, 1], p_recv.at[back(j), 1], z * slab + t),
+        )
+
+    for j in range(slab - 1, 0, -1):
+        for copy in part(j):
+            copy.start()
+    own_part = [
+        pltpu.make_async_copy(gacc.at[s], racc.at[s], local_sem.at[1]),
+        pltpu.make_async_copy(gml.at[s], rml.at[s], local_sem.at[2]),
+    ]
+    for copy in own_part:
+        copy.start()
+
+    for copy in loads:
+        copy.wait()
+    own_att.wait()
+    for j in range(1, slab):
+        for group in range(groups):
+            at = pl.ds(pl.multiple_of(peer(j) * text_cols + group * width, 128), width)
+            arrived(att.at[:, at], o_recv.at[j, group])
+
+    step = 16
+
+    def main_rows(i, _):
+        at = pl.ds(pl.multiple_of(i * step, step), step)
+        summed = v_hidden[at, :].astype(jnp.float32) + att[at, :].astype(jnp.float32)
+        v_shaped[at, :] = shaped_rows(summed, v_mmod[...])
+        return 0
+
+    lax.fori_loop(0, rows // step, main_rows, 0)
+    main_velocity = jnp.dot(v_shaped[...], v_mhead[...], preferred_element_type=jnp.float32)
+
+    for copy in own_part:
+        copy.wait()
+    for j in range(1, slab):
+        arrived(racc.at[peer(j)], p_recv.at[j, 0])
+        arrived(rml.at[peer(j)], p_recv.at[j, 1])
+
+    pieces = []
+    for core in range(cores):
+        members = range(core, slab, cores)
+        for h in range(guide_heads):
+            peaks = [rml[t, :, h : h + 1] for t in members]
+            totals = [rml[t, :, guide_heads + h : guide_heads + h + 1] for t in members]
+            peak = functools.reduce(jnp.maximum, peaks)
+            factors = [jnp.exp2((p - peak) * scale) for p in peaks]
+            total = sum(f * l for f, l in zip(factors, totals))
+            summed = sum(
+                f * racc[t, :, h * HDIM : (h + 1) * HDIM] for f, t in zip(factors, members)
+            )
+            pieces.append((summed / total).astype(jnp.bfloat16))
+    guide_attended = jnp.concatenate(pieces, axis=-1)
+    guide_sum = v_ghidden[...].astype(jnp.float32) + jnp.dot(
+        guide_attended, v_gout[...], preferred_element_type=jnp.float32
+    )
+    v_gshaped[...] = shaped_rows(guide_sum, v_gmod[...])
+    guide_velocity = jnp.dot(v_gshaped[...], v_ghead[...], preferred_element_type=jnp.float32)
+    result = guide_velocity + guidance_scale[0] * (main_velocity - guide_velocity)
+    now = step_index[0]
+    velocity[...] = result
+    next_latent[...] = v_latent[...] + (sigma_table[now + 1] - sigma_table[now]) * result
+
+    for j in range(1, slab):
+        for kv in range(2):
+            slab_text(j, kv).wait_send()
+            if j < cores:
+                slab_guide(j, kv).wait_send()
+        for copy in slab_query(j):
+            copy.wait_send()
+        for group in range(groups):
+            give(j, group).wait_send()
+        for copy in part(j):
+            copy.wait_send()
+    for goes, make in sent:
+
+        @pl.when(goes)
+        def _(make=make):
+            for copy in make():
+                copy.wait_send()
+
+
+def fused(slabs, slab, cores, *args):
+    (
+        latent,
+        main_hidden,
+        main_query,
+        text_key,
+        text_value,
+        text_len,
+        guide_hidden,
+        guide_query,
+        guide_key,
+        guide_value,
+        guide_out,
+        main_head,
+        guide_head,
+        main_modulation,
+        guide_modulation,
+        guidance_scale,
+        sigma_table,
+        step_index,
+    ) = args
+    rows, width = main_query.shape
+    text_rows = text_key.shape[0]
+    guide_width = guide_query.shape[1]
+    text_cols = width // slab
+    guide_cols = guide_width // cores
+    bf16, f32 = jnp.bfloat16, jnp.float32
+    dma = pltpu.SemaphoreType.DMA
+    like = lambda x: pltpu.VMEM(x.shape, x.dtype)
+    scratch = [
+        pltpu.VMEM((slabs, slab, text_rows, text_cols), bf16),
+        pltpu.VMEM((slabs, slab, text_rows, text_cols), bf16),
+        pltpu.VMEM((slab, rows, text_cols), bf16),
+        pltpu.VMEM((slab, rows, text_cols), bf16),
+        pltpu.VMEM((rows, width), bf16),
+        pltpu.VMEM((slabs, cores, rows, guide_cols), bf16),
+        pltpu.VMEM((slabs, cores, rows, guide_cols), bf16),
+        pltpu.VMEM((slab, rows, guide_cols), bf16),
+        pltpu.VMEM((slab, rows, guide_cols), f32),
+        pltpu.VMEM((slab, rows, 128), f32),
+        pltpu.VMEM((slab, rows, guide_cols), f32),
+        pltpu.VMEM((slab, rows, 128), f32),
+        like(latent),
+        like(main_hidden),
+        like(guide_hidden),
+        like(guide_out),
+        like(main_head),
+        like(guide_head),
+        like(main_modulation),
+        like(guide_modulation),
+        pltpu.VMEM(main_hidden.shape, bf16),
+        pltpu.VMEM(guide_hidden.shape, bf16),
+        dma((6,)),
+        dma((8,)),
+        dma((slab, 2)),
+        dma((slab, 2)),
+        dma((slab, 2)),
+        dma((slab, 2)),
+        dma((cores, 2)),
+        dma((cores, 2)),
+        dma((2, slab, 2)),
+        dma((2, slab, 2)),
+        dma((2, slabs, 2)),
+        dma((2, slabs, 2)),
+        dma((2, slabs, 2)),
+        dma((2, slabs, 2)),
+        dma((slab, 2)),
+        dma((slab, 2)),
+        dma((slab, 2)),
+        dma((slab, 2)),
+    ]
+    keys, guide_keys = slabs * slab * text_rows, slabs * cores * rows
+    out = jax.ShapeDtypeStruct(latent.shape, f32)
+    return pl.pallas_call(
+        functools.partial(kernel, slabs, slab, cores),
+        out_shape=(out, out),
+        in_specs=[pl.BlockSpec(memory_space=pltpu.SMEM)] * 4
+        + [pl.BlockSpec(memory_space=pl.ANY)] * 14,
+        out_specs=[pl.BlockSpec(memory_space=pltpu.VMEM)] * 2,
+        scratch_shapes=scratch,
+        compiler_params=pltpu.CompilerParams(
+            collective_id=0, has_side_effects=True, vmem_limit_bytes=48 * 1024 * 1024
+        ),
+        cost_estimate=pl.CostEstimate(
+            flops=4 * rows * (keys * width + guide_keys * guide_width * slab // cores),
+            bytes_accessed=2 * (2 * text_rows + 2 * rows) * width,
+            transcendentals=rows * keys * width // HDIM,
+        ),
+    )(
+        text_len,
+        guidance_scale,
+        sigma_table,
+        step_index,
+        latent,
+        main_hidden,
+        main_query,
+        text_key,
+        text_value,
+        guide_hidden,
+        guide_query,
+        guide_key,
+        guide_value,
+        guide_out,
+        main_head,
+        guide_head,
+        main_modulation,
+        guide_modulation,
+    )
+
+
+def choose(count, slab, cores, *args):
+    rows, width = args[2].shape
+    text_rows = args[3].shape[0]
+    guide_width = args[7].shape[1]
+    fits = (
+        slab > 1
+        and cores > 1
+        and count % slab == 0
+        and slab % cores == 0
+        and count > slab
+        and rows % 16 == 0
+        and text_rows % 16 == 0
+        and width % (slab * HDIM) == 0
+        and guide_width % (cores * HDIM) == 0
+    )
+    if fits:
+        return fused(count // slab, slab, cores, *args)
+    return per_device(*args)
+
+
 def solution(mesh):
     placed = (
         P(("parts", "seq"), None),
@@ -127,8 +747,9 @@
         P(),
         P("parts"),
     )
+    slab, cores = layout(mesh)
     return jax.shard_map(
-        per_device,
+        functools.partial(choose, mesh.shape["seq"], slab, cores),
         mesh=mesh,
         in_specs=placed,
         out_specs=(P(("parts", "seq"), None), P(("parts", "seq"), None)),

time: 236 us -> 101 us (0.43)
  waiting for transfers between devices: 167 us -> 0 us
  Pallas kernels: 0 us -> 85 us
  matrix products: 16.1 us -> 0 us
  local copies, waits for them, and re-layouts: 27.9 us -> 12.6 us
  between operations: 17.1 us -> 2.85 us
  other arithmetic: 7.15 us -> 0 us
    all_gather x4 -> x0, waiting for transfers between devices: 165 us -> none  [the longest x1 47.5 us: per_device(): all_text_keys = lax.all_gather(text_key, 'seq', axis=0, tiled=True)]
    pallas_call x0 -> x1, Pallas kernels: none -> 85 us  [fused(): pl.pallas_call(functools.partial(kernel, slabs, slab, cores), out_shape=(...]
    all_gather x4 -> x0, local copies, waits for them, and re-layouts: 24.5 us -> none  [the longest x1 7.95 us: per_device(): all_text_keys = lax.all_gather(text_key, 'seq', axis=0, tiled=True)]
    dot_general x7 -> x0, matrix products: 16.1 us -> none  [the longest x2 7.28 us: fold_step(): jnp.einsum('hqk,khd->hqd', weights.astype(jnp.bfloat16), value_heads, pre...]
    unnamed x20 -> x29, local copies, waits for them, and re-layouts: 3.39 us -> 9.65 us
    reduce_sum x6 -> x0, other arithmetic: 5.39 us -> none  [the longest x2 3.08 us: fold_step(): totals = jnp.sum(weights, axis=-1)]
    pallas_call x0 -> x2, local copies, waits for them, and re-layouts: none -> 2.99 us  [fused(): pl.pallas_call(functools.partial(kernel, slabs, slab, cores), out_shape=(...]
    unnamed x4 -> x0, waiting for transfers between devices: 2.58 us -> none
  transfers between devices with their start and end apart: 4 -> 0, of which waited for: 4 -> 0; matrix products, arithmetic and copies ran while one was open for 13% -> 0% of each run, Pallas kernels for 0% -> 0%
where the time goes in v1:
time: 101 us; the launch traced here: 100 us
  Pallas kernels  85 us (84%)
  local copies, waits for them, and re-layouts  12.6 us (12%)
  between operations  2.85 us (3%)
    pallas_call x1, Pallas kernels, fused(): pl.pallas_call(functools.partial(kernel, slabs, slab, cores), out_shape=(...  85 us
    unnamed x29, local copies, waits for them, and re-layouts  9.65 us
    pallas_call x2, local copies, waits for them, and re-layouts, fused(): pl.pallas_call(functools.partial(kernel, slabs, slab, cores), out_shape=(...  2.99 us

profile of v1, /device:TPU:0, one launch (start us, length us, event | category | flops | bytes accessed | tf_op | source)
XLA Modules:
  0.0 100.4 jit_solution(1606930292725810842)
XLA Ops:
  0.6 0.0 copy-start.12
  0.6 0.0 copy-start.11
  0.7 0.0 copy-start.5
  0.7 0.0 copy-start.3
  0.7 0.0 copy-start.2
  0.7 0.0 copy-start
  2.8 0.8 copy.20.latent
  3.6 1.2 %copy.22.guide_head = bf16[1536,64]{1,0:T(8,128)(2,1)S(1)} copy(bf16[1536,64]{0,1:T(8,128)(2,1)} %param.30) | data formatting | bytes 393216 | tf_op args[12]
  4.8 1.7 %copy.21.main_head = bf16[5120,64]{1,0:T(8,128)(2,1)S(1)} copy(bf16[5120,64]{0,1:T(8,128)(2,1)} %param.29) | data formatting | bytes 1310720 | tf_op args[11]
  6.4 0.0 copy-done.12
  6.4 0.0 copy-done.11
  6.4 0.0 copy-done.5
  6.5 0.0 copy-done.3
  6.5 0.0 copy-done.2
  6.5 0.0 copy-done
  6.5 0.0 copy-start.1
  6.5 1.2 %copy-done.1 = bf16[96,5120]{1,0:T(8,128)(2,1)S(1)} copy-done((bf16[96,5120]{1,0:T(8,128)(2,1)S(1)}, bf16[96,5120]{1,0:T(8,128)(2,1)}, u32[]{:S(2)}) %copy-start.1) | copy-done | bytes 983064
  7.7 0.0 copy-start.4
  7.7 1.0 copy-done.4
  8.7 0.0 copy-start.6
  8.7 0.9 copy-done.6
  9.6 0.0 copy-start.7
  9.6 0.9 copy-done.7
  10.5 0.0 copy-start.10
  10.5 0.8 copy-done.10
  11.3 85.0 %shard_map.185 = (f32[96,64]{1,0:T(8,128)S(1)}, f32[96,64]{1,0:T(8,128)S(1)}) custom-call(s32[1]{0:T(128)S(6)} %copy.25.text_len, f32[1]{0:T(128)S(6)} %copy.26.guidance_scale, f32[51]{0:T(128)S(1)} %copy-done.12, s32[1]{0:T(128)S(6)} %copy.27.step_index, f32[96,64]{1,0:T(8,128)S(1)} %copy.20.latent, bf16[96,5120]{1,0:T(8,128)(2,1)S(1)} %copy-done, ...), custom_call_target="tpu_custom_call" | custom-call | flops 1459617792 | bytes 2621440 | tf_op jit(solution)/shard_map/pallas_call | solution.py:672
  96.2 0.0 copy-start.8
  96.2 0.6 copy-done.8
  96.8 0.0 copy-start.9
  96.8 0.6 copy-done.9
  97.4 1.5 %copy.23 = f32[96,64]{0,1:T(8,128)} copy(f32[96,64]{1,0:T(8,128)} %copy-done.9) | data formatting | bytes 49152 | tf_op jit(solution)/shard_map/pallas_call | solution.py:672
  98.9 1.5 %copy.24 = f32[96,64]{0,1:T(8,128)} copy(f32[96,64]{1,0:T(8,128)} %copy-done.8) | data formatting | bytes 49152 | tf_op jit(solution)/shard_map/pallas_call | solution.py:672
Async XLA Ops:
  0.6 5.8 %copy-start.12 = (f32[51]{0:T(128)S(1)}, f32[51]{0:T(128)}, u32[]{:S(2)}) copy-start(f32[51]{0:T(128)} %sigma_table.1) | copy-start | bytes 616
  0.6 5.8 %copy-start.11 = (f32[2,1536]{1,0:T(2,128)S(1)}, f32[2,1536]{1,0:T(2,128)}, u32[]{:S(2)}) copy-start(f32[2,1536]{1,0:T(2,128)} %guide_modulation.1) | copy-start | bytes 36868
  0.7 5.8 %copy-start.5 = (bf16[96,768]{1,0:T(8,128)(2,1)S(1)}, bf16[96,768]{1,0:T(8,128)(2,1)}, u32[]{:S(2)}) copy-start(bf16[96,768]{1,0:T(8,128)(2,1)} %guide_query.1) | copy-start | bytes 442372
  0.7 5.8 %copy-start.3 = (bf16[32,5120]{1,0:T(8,128)(2,1)S(1)}, bf16[32,5120]{1,0:T(8,128)(2,1)}, u32[]{:S(2)}) copy-start(bf16[32,5120]{1,0:T(8,128)(2,1)} %text_value.1) | copy-start | bytes 983044
  0.7 5.8 %copy-start.2 = (bf16[32,5120]{1,0:T(8,128)(2,1)S(1)}, bf16[32,5120]{1,0:T(8,128)(2,1)}, u32[]{:S(2)}) copy-start(bf16[32,5120]{1,0:T(8,128)(2,1)} %text_key.1) | copy-start | bytes 983044
  0.7 5.8 %copy-start = (bf16[96,5120]{1,0:T(8,128)(2,1)S(1)}, bf16[96,5120]{1,0:T(8,128)(2,1)}, u32[]{:S(2)}) copy-start(bf16[96,5120]{1,0:T(8,128)(2,1)} %main_hidden.1) | copy-start | bytes 2949124
  6.5 1.2 %copy-start.1 = (bf16[96,5120]{1,0:T(8,128)(2,1)S(1)}, bf16[96,5120]{1,0:T(8,128)(2,1)}, u32[]{:S(2)}) copy-start(bf16[96,5120]{1,0:T(8,128)(2,1)} %main_query.1) | copy-start | bytes 2949124
  7.7 1.0 copy-start.4
  8.7 0.9 copy-start.6
  9.6 0.9 copy-start.7
  10.5 0.8 copy-start.10
  96.2 0.6 copy-start.8
  96.8 0.6 copy-start.9

commit v2 on v1

--- a/solution.py
+++ b/solution.py
@@ -132,6 +132,10 @@
     return (normed * (1.0 + modulation[1:2]) + modulation[0:1]).astype(jnp.bfloat16)
 
 
+def across(a, b):
+    return lax.dot_general(a, b, (((1,), (1,)), ((), ())), preferred_element_type=jnp.float32)
+
+
 def kernel(
     slabs,
     slab,
@@ -140,7 +144,6 @@
     guidance_scale,
     sigma_table,
     step_index,
-    latent,
     main_hidden,
     main_query,
     text_key,
@@ -154,8 +157,9 @@
     guide_head,
     main_modulation,
     guide_modulation,
-    velocity,
-    next_latent,
+    plain,
+    guided,
+    change,
     tk,
     tv,
     tq,
@@ -168,7 +172,6 @@
     gml,
     racc,
     rml,
-    v_latent,
     v_hidden,
     v_ghidden,
     v_gout,
@@ -246,7 +249,6 @@
         (guide_hidden, v_ghidden),
         (guide_head, v_ghead),
         (guide_modulation, v_gmod),
-        (latent, v_latent),
     ]
     loads = [pltpu.make_async_copy(a, b, load_sem.at[i]) for i, (a, b) in enumerate(loads)]
     for copy in mine:
@@ -445,9 +447,7 @@
     bias = jnp.where(positions < text_len[0], 0.0, -1e30).astype(jnp.float32)
 
     def weigh(q, k, bias=None):
-        scores = lax.dot_general(
-            q, k, (((1,), (1,)), ((), ())), preferred_element_type=jnp.float32
-        )
+        scores = across(q, k)
         if bias is not None:
             scores = scores + bias
         peak = jnp.max(scores, axis=-1, keepdims=True)
@@ -545,7 +545,7 @@
         return 0
 
     lax.fori_loop(0, rows // step, main_rows, 0)
-    main_velocity = jnp.dot(v_shaped[...], v_mhead[...], preferred_element_type=jnp.float32)
+    main_velocity = across(v_mhead[...], v_shaped[...])
 
     for copy in own_part:
         copy.wait()
@@ -571,11 +571,11 @@
         guide_attended, v_gout[...], preferred_element_type=jnp.float32
     )
     v_gshaped[...] = shaped_rows(guide_sum, v_gmod[...])
-    guide_velocity = jnp.dot(v_gshaped[...], v_ghead[...], preferred_element_type=jnp.float32)
-    result = guide_velocity + guidance_scale[0] * (main_velocity - guide_velocity)
+    guide_velocity = across(v_ghead[...], v_gshaped[...])
     now = step_index[0]
-    velocity[...] = result
-    next_latent[...] = v_latent[...] + (sigma_table[now + 1] - sigma_table[now]) * result
+    plain[...] = guide_velocity
+    guided[...] = guidance_scale[0] * (main_velocity - guide_velocity)
+    change[...] = jnp.full(change.shape, sigma_table[now + 1] - sigma_table[now], jnp.float32)
 
     for j in range(1, slab):
         for kv in range(2):
@@ -617,6 +617,7 @@
         sigma_table,
         step_index,
     ) = args
+    main_head, guide_head = main_head.T, guide_head.T
     rows, width = main_query.shape
     text_rows = text_key.shape[0]
     guide_width = guide_query.shape[1]
@@ -638,7 +639,6 @@
         pltpu.VMEM((slab, rows, 128), f32),
         pltpu.VMEM((slab, rows, guide_cols), f32),
         pltpu.VMEM((slab, rows, 128), f32),
-        like(latent),
         like(main_hidden),
         like(guide_hidden),
         like(guide_out),
@@ -649,7 +649,7 @@
         pltpu.VMEM(main_hidden.shape, bf16),
         pltpu.VMEM(guide_hidden.shape, bf16),
         dma((6,)),
-        dma((8,)),
+        dma((7,)),
         dma((slab, 2)),
         dma((slab, 2)),
         dma((slab, 2)),
@@ -668,16 +668,16 @@
         dma((slab, 2)),
     ]
     keys, guide_keys = slabs * slab * text_rows, slabs * cores * rows
-    out = jax.ShapeDtypeStruct(latent.shape, f32)
-    return pl.pallas_call(
+    out = jax.ShapeDtypeStruct(latent.shape[::-1], f32)
+    plain, guided, change = pl.pallas_call(
         functools.partial(kernel, slabs, slab, cores),
-        out_shape=(out, out),
+        out_shape=(out, out, jax.ShapeDtypeStruct((1, rows), f32)),
         in_specs=[pl.BlockSpec(memory_space=pltpu.SMEM)] * 4
-        + [pl.BlockSpec(memory_space=pl.ANY)] * 14,
-        out_specs=[pl.BlockSpec(memory_space=pltpu.VMEM)] * 2,
+        + [pl.BlockSpec(memory_space=pltpu.HBM)] * 13,
+        out_specs=[pl.BlockSpec(memory_space=pltpu.VMEM)] * 3,
         scratch_shapes=scratch,
         compiler_params=pltpu.CompilerParams(
-            collective_id=0, has_side_effects=True, vmem_limit_bytes=48 * 1024 * 1024
+            collective_id=0, has_side_effects=True, vmem_limit_bytes=56 * 1024 * 1024
         ),
         cost_estimate=pl.CostEstimate(
             flops=4 * rows * (keys * width + guide_keys * guide_width * slab // cores),
@@ -689,7 +689,6 @@
         guidance_scale,
         sigma_table,
         step_index,
-        latent,
         main_hidden,
         main_query,
         text_key,
@@ -704,6 +703,8 @@
         main_modulation,
         guide_modulation,
     )
+    velocity = plain + guided
+    return velocity.T, (latent.T + change * velocity).T
 
 
 def choose(count, slab, cores, *args):

time: 101 us -> 90.3 us (0.89)
  local copies, waits for them, and re-layouts: 12.6 us -> 0.01 us
  other arithmetic: 0 us -> 1.41 us
    unnamed x29 -> x2, local copies, waits for them, and re-layouts: 9.65 us -> 0.01 us
    pallas_call x2 -> x0, local copies, waits for them, and re-layouts: 2.99 us -> none  [fused(): pl.pallas_call(functools.partial(kernel, slabs, slab, cores), out_shape=(...]
    transpose x0 -> x1, other arithmetic: none -> 1.41 us  [fused(): return (velocity.T, (latent.T + change * velocity).T)]
    pallas_call x1, Pallas kernels: 85 us -> 86 us  [fused(): pl.pallas_call(functools.partial(kernel, slabs, slab, cores), out_shape=(...]
where the time goes in v2:
time: 90.3 us; the launch traced here: 90.1 us
  Pallas kernels  86 us (95%)
  between operations  2.6 us (3%)
  other arithmetic  1.41 us (2%)
    pallas_call x1, Pallas kernels, fused(): pl.pallas_call(functools.partial(kernel, slabs, slab, cores), out_shape=(...  86 us

profile of v2, /device:TPU:0, one launch (start us, length us, event | category | flops | bytes accessed | tf_op | source)
XLA Modules:
  0.0 90.1 jit_solution(1973050442488608681)
XLA Ops:
  2.6 0.0 copy-start
  2.6 86.0 %shard_map.185 = (f32[64,96]{1,0:T(8,128)}, f32[64,96]{1,0:T(8,128)}, f32[1,96]{1,0:T(1,128)}) custom-call(s32[1]{0:T(128)S(6)} %copy.20.text_len, f32[1]{0:T(128)S(6)} %copy.21.guidance_scale, f32[51]{0:T(128)} %sigma_table.1, s32[1]{0:T(128)S(6)} %copy.22.step_index, bf16[96,5120]{1,0:T(8,128)(2,1)} %main_hidden.1, bf16[96,5120]{1,0:T(8,128)(2,1)} %main_query.1, ...), custom_call_target="tpu_custom_call" | custom-call | flops 1459617792 | bytes 2621440 | tf_op jit(solution)/shard_map/pallas_call | solution.py:672
  88.6 0.0 copy-done
  88.6 1.4 %fusion = (f32[96,64]{0,1:T(8,128)}, f32[96,64]{0,1:T(8,128)}) fusion(f32[96,64]{0,1:T(8,128)S(1)} %copy-done, f32[96]{0:T(128)} %bitcast.13, f32[64,96]{1,0:T(8,128)} %get-tuple-element.5, f32[64,96]{1,0:T(8,128)} %get-tuple-element.6), kind=kLoop, calls=%fused_computation.1 | loop fusion | flops 18432 | bytes 123264 | tf_op jit(solution)/shard_map/transpose | solution.py:707
Async XLA Ops:
  2.6 86.1 %copy-start = (f32[96,64]{0,1:T(8,128)S(1)}, f32[96,64]{0,1:T(8,128)}, u32[]{:S(2)}) copy-start(f32[96,64]{0,1:T(8,128)} %param.18) | copy-start | bytes 73732

commit v3 on v2

--- a/solution.py
+++ b/solution.py
@@ -165,6 +165,8 @@
     tq,
     to,
     att,
+    hq,
+    ho,
     gk,
     gv,
     gq,
@@ -199,6 +201,10 @@
     o_recv,
     p_send,
     p_recv,
+    hq_send,
+    hq_recv,
+    ho_send,
+    ho_recv,
 ):
     me = lax.axis_index("seq")
     z = me // slab
@@ -211,6 +217,11 @@
     guide_heads = guide_cols // HDIM
     keys = slabs * slab * tk.shape[2]
     guide_keys = slabs * cores * rows
+    width = text_cols // 2
+    end = jnp.logical_or(z == 0, z == slabs - 1)
+    host = jnp.logical_or(z == 1, z == slabs - 2)
+    inner = jnp.where(z == 0, 1, slabs - 2) * slab
+    outer = jnp.where(z == 1, 0, slabs - 1) * slab
     scale = HDIM ** (-0.5) * math.log2(math.e)
 
     def cols(ref, index, width):
@@ -264,30 +275,53 @@
     for j in range(1, slab):
         greet(z * slab + peer(j))
 
-    @pl.when(z > 0)
+    @pl.when(end)
     def _():
-        greet(me - slab)
-
-    @pl.when(z < slabs - 1)
+        for t in range(slab):
+            greet(inner + t)
+
+    @pl.when(host)
     def _():
-        greet(me + slab)
-
-    ends = jnp.where(z > 0, 1, 0) + jnp.where(z < slabs - 1, 1, 0)
-    pl.semaphore_wait(barrier, slab - 1 + ends)
+        for t in range(slab):
+            greet(outer + t)
+
+    @pl.when(z > 1)
+    def _():
+        @pl.when(z < slabs - 1)
+        def _():
+            greet(me - slab)
+
+    @pl.when(z < slabs - 2)
+    def _():
+        @pl.when(z > 0)
+        def _():
+            greet(me + slab)
+
+    greeted = jnp.where(end, slab, 0) + jnp.where(host, slab, 0)
+    greeted += jnp.where(jnp.logical_and(z > 1, z < slabs - 1), 1, 0)
+    greeted += jnp.where(jnp.logical_and(z < slabs - 2, z > 0), 1, 0)
+    pl.semaphore_wait(barrier, slab - 1 + greeted)
 
     target = (me - slab, me + slab)
     has_target = (z > 0, z < slabs - 1)
+    target_end = (z == 1, z == slabs - 2)
+    target_takes = tuple(
+        jnp.logical_and(has, jnp.logical_not(is_end)) for has, is_end in zip(has_target, target_end)
+    )
     sent = []
 
-    def both_ways(make):
+    def send_if(goes, make):
+        @pl.when(goes)
+        def _():
+            for copy in make():
+                copy.start()
+
+        sent.append((goes, make))
+
+    def both_ways(make, group=1):
         for way in range(2):
-
-            @pl.when(has_target[way])
-            def _(way=way):
-                for copy in make(way):
-                    copy.start()
-
-            sent.append((has_target[way], functools.partial(make, way)))
+            goes = has_target[way] if group == 1 else target_takes[way]
+            send_if(goes, functools.partial(make, way))
 
     both = ((text_key, tk), (text_value, tv))
     guide_both = ((guide_key, gk), (guide_value, gv))
@@ -303,12 +337,26 @@
             z * slab + t,
         )
 
-    def chain_own(j, kv, way):
+    def half(place, group):
+        return place.at[:, pl.ds(group * width, width)]
+
+    def halves(place, group):
+        return place.at[:, :, pl.ds(group * width, width)]
+
+    def chain_own(j, kv, group, way):
         source, place = both[kv]
         t = peer(j)
-        src = cols(source, s, text_cols) if j == 0 else place.at[z, t]
+        if j == 0:
+            src = cols(source, s * 2 + group, width)
+        else:
+            src = half(place.at[z, t], group)
+        unit = kv * 2 + group
         return remote(
-            src, place.at[z, t], own_send.at[way, j, kv], near_recv.at[way, j, kv], target[way]
+            src,
+            half(place.at[z, t], group),
+            own_send.at[way, j, unit],
+            near_recv.at[way, j, unit],
+            target[way],
         )
 
     def slab_guide(j, kv):
@@ -322,35 +370,43 @@
             z * slab + t,
         )
 
-    def slab_query(j):
+    def slab_query(j, group):
         t = peer(j)
-        return (
-            remote(
-                cols(main_query, t, text_cols),
-                tq.at[s],
-                q_send.at[j, 0],
-                q_recv.at[back(j), 0],
-                z * slab + t,
-            ),
-            remote(
-                cols(guide_query, t % cores, guide_cols),
-                gq.at[s],
-                q_send.at[j, 1],
-                q_recv.at[back(j), 1],
-                z * slab + t,
-            ),
-        )
+        return remote(
+            cols(main_query, t * 2 + group, width),
+            half(tq.at[s], group),
+            q_send.at[j, group],
+            q_recv.at[back(j), group],
+            z * slab + t,
+        )
+
+    def slab_guide_query(j):
+        t = peer(j)
+        return remote(
+            cols(guide_query, t % cores, guide_cols),
+            gq.at[s],
+            q_send.at[j, 2],
+            q_recv.at[back(j), 2],
+            z * slab + t,
+        )
+
+    def lend(t):
+        return remote(
+            cols(main_query, t * 2, width), hq.at[s], hq_send.at[t], hq_recv.at[s], inner + t
+        )
+
+    def repay(t):
+        at = pl.ds(pl.multiple_of(s * text_cols, 128), width)
+        return remote(ho.at[t], att.at[:, at], ho_send.at[t], ho_recv.at[s], outer + t)
 
     for kv in range(2):
         for j in range(slab - 1, 0, -1):
             slab_text(j, kv).start()
-        both_ways(lambda way, kv=kv: [chain_own(0, kv, way)])
+        for group in range(2):
+            both_ways(lambda way, kv=kv, group=group: [chain_own(0, kv, group, way)], group)
     for kv in range(2):
         for j in range(1, cores):
             slab_guide(j, kv).start()
-    for j in range(slab - 1, 0, -1):
-        for copy in slab_query(j):
-            copy.start()
     for copy in loads:
         copy.start()
 
@@ -361,7 +417,17 @@
         place = both[kv][1]
         for j in range(1, slab):
             arrived(place.at[z, peer(j)], t_recv.at[j, kv])
-            both_ways(lambda way, kv=kv, j=j: [chain_own(j, kv, way)])
+            for group in range(2):
+                both_ways(
+                    lambda way, kv=kv, j=j, group=group: [chain_own(j, kv, group, way)], group
+                )
+    send_if(end, lambda: [lend(t) for t in range(slab)])
+    for j in range(slab - 1, 0, -1):
+        slab_query(j, 1).start()
+    others = [j for j in range(slab - 1, 0, -1)]
+    send_if(jnp.logical_not(end), lambda: [slab_query(j, 0) for j in others])
+    for j in others:
+        slab_guide_query(j).start()
     for copy in mine:
         copy.wait()
     for kv in range(2):
@@ -382,66 +448,65 @@
 
     both_ways(lambda way: [guide_chain(0, 0, way), guide_chain(0, 1, way)])
 
-    def text_chain(d, kv, way):
-        place = both[kv][1]
+    def text_chain(d, kv, group, way):
         from_z = z + d if way == 0 else z - d
+        block = halves(both[kv][1].at[from_z], group)
+        unit = kv * 2 + group
         return remote(
-            place.at[from_z],
-            place.at[from_z],
-            fwd_send.at[way, d, kv],
-            far_recv.at[way, d, kv],
-            target[way],
-        )
+            block, block, fwd_send.at[way, d, unit], far_recv.at[way, d, unit], target[way]
+        )
+
+    def coming(d, way):
+        return z + d < slabs if way == 0 else z - d >= 0
 
     for d in range(1, slabs):
         for kv in range(2):
             place = both[kv][1]
             for way in range(2):
                 from_z = z + d if way == 0 else z - d
-                comes = from_z < slabs if way == 0 else from_z >= 0
-
-                @pl.when(comes)
-                def _(way=way, kv=kv, d=d, place=place, from_z=from_z):
-                    if d == 1:
-                        for j in range(slab):
-                            arrived(place.at[from_z, peer(j)], near_recv.at[way, j, kv])
-                    else:
-                        arrived(place.at[from_z], far_recv.at[way, d - 1, kv])
-
-                if d < slabs - 1:
-                    goes = jnp.logical_and(comes, has_target[way])
-
-                    @pl.when(goes)
-                    def _(way=way, kv=kv, d=d):
-                        text_chain(d, kv, way).start()
-
-                    sent.append((goes, lambda way=way, kv=kv, d=d: [text_chain(d, kv, way)]))
+                for group in range(2):
+                    comes = coming(d, way)
+                    if group == 0:
+                        comes = jnp.logical_and(comes, jnp.logical_not(end))
+
+                    @pl.when(comes)
+                    def _(way=way, kv=kv, d=d, group=group, place=place, from_z=from_z):
+                        unit = kv * 2 + group
+                        if d == 1:
+                            for j in range(slab):
+                                arrived(
+                                    half(place.at[from_z, peer(j)], group),
+                                    near_recv.at[way, j, unit],
+                                )
+                        else:
+                            arrived(
+                                halves(place.at[from_z], group), far_recv.at[way, d - 1, unit]
+                            )
+
+                    if d < slabs - 1:
+                        takes = has_target[way] if group == 1 else target_takes[way]
+                        send_if(
+                            jnp.logical_and(comes, takes),
+                            lambda way=way, kv=kv, d=d, group=group: [
+                                text_chain(d, kv, group, way)
+                            ],
+                        )
 
     def guide_arrived(d, way):
         from_z = z + d if way == 0 else z - d
         for kv in range(2):
             arrived(guide_both[kv][1].at[from_z], gc_recv.at[way, d - 1, kv])
 
-    for d in range(1, slabs):
+    def pass_guide(d):
         for way in range(2):
-            comes = z + d < slabs if way == 0 else z - d >= 0
-            goes = jnp.logical_and(comes, has_target[way])
+            goes = jnp.logical_and(coming(d, way), has_target[way])
 
             @pl.when(goes)
-            def _(way=way, d=d):
+            def _(way=way):
                 guide_arrived(d, way)
-                if d < slabs - 1:
-                    for kv in range(2):
-                        guide_chain(d, kv, way).start()
 
             if d < slabs - 1:
-                sent.append(
-                    (goes, lambda way=way, d=d: [guide_chain(d, kv, way) for kv in range(2)])
-                )
-
-    for j in range(1, slab):
-        arrived(tq.at[peer(j)], q_recv.at[j, 0])
-        arrived(gq.at[peer(j)], q_recv.at[j, 1])
+                send_if(goes, lambda way=way: [guide_chain(d, kv, way) for kv in range(2)])
 
     positions = lax.broadcasted_iota(jnp.int32, (1, keys), 1)
     bias = jnp.where(positions < text_len[0], 0.0, -1e30).astype(jnp.float32)
@@ -454,37 +519,66 @@
         weights = jnp.exp2((scores - peak) * scale)
         return peak, weights, jnp.sum(weights, axis=-1, keepdims=True)
 
-    groups = 2 if heads % 2 == 0 else 1
-    width = text_cols // groups
-
     def give(j, group):
         t = peer(j)
         at = pl.ds(pl.multiple_of(s * text_cols + group * width, 128), width)
         return remote(
-            to.at[t, :, pl.ds(group * width, width)],
+            half(to.at[t], group),
             att.at[:, at],
             o_send.at[j, group],
             o_recv.at[back(j), group],
             z * slab + t,
         )
 
-    for group in range(groups):
-
+    def text_heads(group, queries, results, first):
         def one_head(h, _):
             at = pl.ds(pl.multiple_of(group * width + h * HDIM, 128), HDIM)
+            to_at = pl.ds(pl.multiple_of(first + h * HDIM, 128), HDIM)
             k = tk[:, :, :, at].reshape(keys, HDIM)
             v = tv[:, :, :, at].reshape(keys, HDIM)
-            for t in range(slab):
-                _, weights, total = weigh(tq[t, :, at], k, bias)
-                out = jnp.dot(weights.astype(jnp.bfloat16), v, preferred_element_type=jnp.float32)
-                to[t, :, at] = (out / total).astype(jnp.bfloat16)
+            q = queries[:, :, to_at].reshape(slab * rows, HDIM)
+            _, weights, total = weigh(q, k, bias)
+            out = jnp.dot(weights.astype(jnp.bfloat16), v, preferred_element_type=jnp.float32)
+            out = (out / total).astype(jnp.bfloat16)
+            results[:, :, to_at] = out.reshape(slab, rows, HDIM)
             return 0
 
-        lax.fori_loop(0, heads // groups, one_head, 0)
-        for j in range(slab - 1, 0, -1):
-            give(j, group).start()
-    own_att = pltpu.make_async_copy(to.at[s], cols(att, s, text_cols), local_sem.at[0])
-    own_att.start()
+        lax.fori_loop(0, heads // 2, one_head, 0)
+
+    @pl.when(host)
+    def _():
+        for t in range(slab):
+            arrived(hq.at[t], hq_recv.at[t])
+        text_heads(0, hq, ho, 0)
+
+    send_if(host, lambda: [repay(t) for t in range(slab)])
+    for d in range(1, slabs - 2):
+        pass_guide(d)
+
+    @pl.when(jnp.logical_not(end))
+    def _():
+        for j in range(1, slab):
+            arrived(half(tq.at[peer(j)], 0), q_recv.at[j, 0])
+        text_heads(0, tq, to, 0)
+
+    send_if(jnp.logical_not(end), lambda: [give(j, 0) for j in others])
+    for d in range(slabs - 2, slabs - 1):
+        pass_guide(d)
+    for j in range(1, slab):
+        arrived(half(tq.at[peer(j)], 1), q_recv.at[j, 1])
+        arrived(gq.at[peer(j)], q_recv.at[j, 2])
+    text_heads(1, tq, to, width)
+    for j in others:
+        give(j, 1).start()
+    own_att = [
+        pltpu.make_async_copy(half(to.at[s], group), cols(att, s * 2 + group, width), local_sem.at[3 * group])
+        for group in range(2)
+    ]
+    own_att[1].start()
+
+    @pl.when(jnp.logical_not(end))
+    def _():
+        own_att[0].start()
 
     for d in range(1, slabs):
         for way in range(2):
@@ -498,18 +592,13 @@
     for h in range(guide_heads):
         at = pl.ds(h * HDIM, HDIM)
 
-        def one_owner(t, _):
-            k = gk[:, :, :, at].reshape(guide_keys, HDIM)
-            v = gv[:, :, :, at].reshape(guide_keys, HDIM)
-            peak, weights, total = weigh(gq[t, :, at], k)
-            gacc[t, :, at] = jnp.dot(
-                weights.astype(jnp.bfloat16), v, preferred_element_type=jnp.float32
-            )
-            gml[t, :, h : h + 1] = peak
-            gml[t, :, guide_heads + h : guide_heads + h + 1] = total
-            return 0
-
-        lax.fori_loop(0, slab, one_owner, 0)
+        k = gk[:, :, :, at].reshape(guide_keys, HDIM)
+        v = gv[:, :, :, at].reshape(guide_keys, HDIM)
+        peak, weights, total = weigh(gq[:, :, at].reshape(slab * rows, HDIM), k)
+        out = jnp.dot(weights.astype(jnp.bfloat16), v, preferred_element_type=jnp.float32)
+        gacc[:, :, at] = out.reshape(slab, rows, HDIM)
+        gml[:, :, h : h + 1] = peak.reshape(slab, rows, 1)
+        gml[:, :, guide_heads + h : guide_heads + h + 1] = total.reshape(slab, rows, 1)
 
     def part(j):
         t = peer(j)
@@ -530,11 +619,20 @@
 
     for copy in loads:
         copy.wait()
-    own_att.wait()
+    own_att[1].wait()
     for j in range(1, slab):
-        for group in range(groups):
-            at = pl.ds(pl.multiple_of(peer(j) * text_cols + group * width, 128), width)
-            arrived(att.at[:, at], o_recv.at[j, group])
+        arrived(cols(att, peer(j) * 2 + 1, width), o_recv.at[j, 1])
+
+    @pl.when(jnp.logical_not(end))
+    def _():
+        own_att[0].wait()
+        for j in range(1, slab):
+            arrived(cols(att, peer(j) * 2, width), o_recv.at[j, 0])
+
+    @pl.when(end)
+    def _():
+        for t in range(slab):
+            arrived(cols(att, t * 2, width), ho_recv.at[t])
 
     step = 16
 
@@ -582,10 +680,9 @@
             slab_text(j, kv).wait_send()
             if j < cores:
                 slab_guide(j, kv).wait_send()
-        for copy in slab_query(j):
-            copy.wait_send()
-        for group in range(groups):
-            give(j, group).wait_send()
+        slab_query(j, 1).wait_send()
+        slab_guide_query(j).wait_send()
+        give(j, 1).wait_send()
         for copy in part(j):
             copy.wait_send()
     for goes, make in sent:
@@ -632,6 +729,8 @@
         pltpu.VMEM((slab, rows, text_cols), bf16),
         pltpu.VMEM((slab, rows, text_cols), bf16),
         pltpu.VMEM((rows, width), bf16),
+        pltpu.VMEM((slab, rows, text_cols // 2), bf16),
+        pltpu.VMEM((slab, rows, text_cols // 2), bf16),
         pltpu.VMEM((slabs, cores, rows, guide_cols), bf16),
         pltpu.VMEM((slabs, cores, rows, guide_cols), bf16),
         pltpu.VMEM((slab, rows, guide_cols), bf16),
@@ -652,20 +751,24 @@
         dma((7,)),
         dma((slab, 2)),
         dma((slab, 2)),
-        dma((slab, 2)),
-        dma((slab, 2)),
+        dma((slab, 3)),
+        dma((slab, 3)),
         dma((cores, 2)),
         dma((cores, 2)),
-        dma((2, slab, 2)),
-        dma((2, slab, 2)),
-        dma((2, slabs, 2)),
-        dma((2, slabs, 2)),
+        dma((2, slab, 4)),
+        dma((2, slab, 4)),
+        dma((2, slabs, 4)),
+        dma((2, slabs, 4)),
         dma((2, slabs, 2)),
         dma((2, slabs, 2)),
         dma((slab, 2)),
         dma((slab, 2)),
         dma((slab, 2)),
         dma((slab, 2)),
+        dma((slab,)),
+        dma((slab,)),
+        dma((slab,)),
+        dma((slab,)),
     ]
     keys, guide_keys = slabs * slab * text_rows, slabs * cores * rows
     out = jax.ShapeDtypeStruct(latent.shape[::-1], f32)
@@ -716,10 +819,10 @@
         and cores > 1
         and count % slab == 0
         and slab % cores == 0
-        and count > slab
+        and count >= 4 * slab
         and rows % 16 == 0
         and text_rows % 16 == 0
-        and width % (slab * HDIM) == 0
+        and width % (2 * slab * HDIM) == 0
         and guide_width % (cores * HDIM) == 0
     )
     if fits:

time: 90.3 us -> 88.9 us (0.984)
  Pallas kernels: 86 us -> 84.6 us
    pallas_call x1, Pallas kernels: 86 us -> 84.6 us  [fused(): pl.pallas_call(functools.partial(kernel, slabs, slab, cores), out_shape=(...]
where the time goes in v3:
time: 88.9 us; the launch traced here: 88.6 us
  Pallas kernels  84.6 us (95%)
  between operations  2.6 us (3%)
  other arithmetic  1.41 us (2%)
    pallas_call x1, Pallas kernels, fused(): pl.pallas_call(functools.partial(kernel, slabs, slab, cores), out_shape=(...  84.6 us

profile of v3, /device:TPU:0, one launch (start us, length us, event | category | flops | bytes accessed | tf_op | source)
XLA Modules:
  0.0 88.6 jit_solution(7427764262119648793)
XLA Ops:
  2.6 0.0 copy-start
  2.6 84.6 %shard_map.185 = (f32[64,96]{1,0:T(8,128)}, f32[64,96]{1,0:T(8,128)}, f32[1,96]{1,0:T(1,128)}) custom-call(s32[1]{0:T(128)S(6)} %copy.20.text_len, f32[1]{0:T(128)S(6)} %copy.21.guidance_scale, f32[51]{0:T(128)} %sigma_table.1, s32[1]{0:T(128)S(6)} %copy.22.step_index, bf16[96,5120]{1,0:T(8,128)(2,1)} %main_hidden.1, bf16[96,5120]{1,0:T(8,128)(2,1)} %main_query.1, ...), custom_call_target="tpu_custom_call" | custom-call | flops 1459617792 | bytes 2621440 | tf_op jit(solution)/shard_map/pallas_call | solution.py:775
  87.2 0.0 copy-done
  87.2 1.4 %fusion = (f32[96,64]{0,1:T(8,128)}, f32[96,64]{0,1:T(8,128)}) fusion(f32[96,64]{0,1:T(8,128)S(1)} %copy-done, f32[96]{0:T(128)} %bitcast.13, f32[64,96]{1,0:T(8,128)} %get-tuple-element.5, f32[64,96]{1,0:T(8,128)} %get-tuple-element.6), kind=kLoop, calls=%fused_computation.1 | loop fusion | flops 18432 | bytes 123264 | tf_op jit(solution)/shard_map/transpose | solution.py:810
Async XLA Ops:
  2.6 84.6 %copy-start = (f32[96,64]{0,1:T(8,128)S(1)}, f32[96,64]{0,1:T(8,128)}, u32[]{:S(2)}) copy-start(f32[96,64]{0,1:T(8,128)} %param.18) | copy-start | bytes 73732

commit v4 on v3

--- a/solution.py
+++ b/solution.py
@@ -167,6 +167,8 @@
     att,
     hq,
     ho,
+    tp,
+    tl,
     gk,
     gv,
     gq,
@@ -399,35 +401,34 @@
         at = pl.ds(pl.multiple_of(s * text_cols, 128), width)
         return remote(ho.at[t], att.at[:, at], ho_send.at[t], ho_recv.at[s], outer + t)
 
-    for kv in range(2):
-        for j in range(slab - 1, 0, -1):
-            slab_text(j, kv).start()
+    others = [j for j in range(slab - 1, 0, -1)]
+
+    def arrived(place, sem):
+        pltpu.make_async_copy(place, place, sem).wait()
+
+    def begin_chain(kv, j):
         for group in range(2):
-            both_ways(lambda way, kv=kv, group=group: [chain_own(0, kv, group, way)], group)
+            both_ways(lambda way, group=group: [chain_own(j, kv, group, way)], group)
+
+    for j in others:
+        slab_text(j, 0).start()
+    begin_chain(0, 0)
     for kv in range(2):
         for j in range(1, cores):
             slab_guide(j, kv).start()
-    for copy in loads:
-        copy.start()
-
-    def arrived(place, sem):
-        pltpu.make_async_copy(place, place, sem).wait()
-
-    for kv in range(2):
-        place = both[kv][1]
-        for j in range(1, slab):
-            arrived(place.at[z, peer(j)], t_recv.at[j, kv])
-            for group in range(2):
-                both_ways(
-                    lambda way, kv=kv, j=j, group=group: [chain_own(j, kv, group, way)], group
-                )
+    for j in range(1, slab):
+        arrived(tk.at[z, peer(j)], t_recv.at[j, 0])
+        begin_chain(0, j)
     send_if(end, lambda: [lend(t) for t in range(slab)])
-    for j in range(slab - 1, 0, -1):
+    for j in others:
         slab_query(j, 1).start()
-    others = [j for j in range(slab - 1, 0, -1)]
     send_if(jnp.logical_not(end), lambda: [slab_query(j, 0) for j in others])
     for j in others:
         slab_guide_query(j).start()
+    for j in others:
+        slab_text(j, 1).start()
+    for copy in loads:
+        copy.start()
     for copy in mine:
         copy.wait()
     for kv in range(2):
@@ -446,7 +447,13 @@
             target[way],
         )
 
-    both_ways(lambda way: [guide_chain(0, 0, way), guide_chain(0, 1, way)])
+    def begin_guide(d):
+        for way in range(2):
+            turn = z + d == slabs - 1 if way == 0 else z == d
+            send_if(
+                jnp.logical_and(turn, has_target[way]),
+                lambda way=way: [guide_chain(0, 0, way), guide_chain(0, 1, way)],
+            )
 
     def text_chain(d, kv, group, way):
         from_z = z + d if way == 0 else z - d
@@ -459,38 +466,38 @@
     def coming(d, way):
         return z + d < slabs if way == 0 else z - d >= 0
 
+    def pass_text(d, kv):
+        place = both[kv][1]
+        for way in range(2):
+            from_z = z + d if way == 0 else z - d
+            for group in range(2):
+                comes = coming(d, way)
+                if group == 0:
+                    comes = jnp.logical_and(comes, jnp.logical_not(end))
+                unit = kv * 2 + group
+
+                @pl.when(comes)
+                def _(way=way, group=group, unit=unit, from_z=from_z):
+                    if d == 1:
+                        for j in range(slab):
+                            arrived(
+                                half(place.at[from_z, peer(j)], group), near_recv.at[way, j, unit]
+                            )
+                    else:
+                        arrived(halves(place.at[from_z], group), far_recv.at[way, d - 1, unit])
+
+                if d < slabs - 1:
+                    takes = has_target[way] if group == 1 else target_takes[way]
+                    send_if(
+                        jnp.logical_and(comes, takes),
+                        lambda way=way, group=group: [text_chain(d, kv, group, way)],
+                    )
+
+    begin_guide(0)
     for d in range(1, slabs):
-        for kv in range(2):
-            place = both[kv][1]
-            for way in range(2):
-                from_z = z + d if way == 0 else z - d
-                for group in range(2):
-                    comes = coming(d, way)
-                    if group == 0:
-                        comes = jnp.logical_and(comes, jnp.logical_not(end))
-
-                    @pl.when(comes)
-                    def _(way=way, kv=kv, d=d, group=group, place=place, from_z=from_z):
-                        unit = kv * 2 + group
-                        if d == 1:
-                            for j in range(slab):
-                                arrived(
-                                    half(place.at[from_z, peer(j)], group),
-                                    near_recv.at[way, j, unit],
-                                )
-                        else:
-                            arrived(
-                                halves(place.at[from_z], group), far_recv.at[way, d - 1, unit]
-                            )
-
-                    if d < slabs - 1:
-                        takes = has_target[way] if group == 1 else target_takes[way]
-                        send_if(
-                            jnp.logical_and(comes, takes),
-                            lambda way=way, kv=kv, d=d, group=group: [
-                                text_chain(d, kv, group, way)
-                            ],
-                        )
+        pass_text(d, 0)
+        if d < slabs - 1:
+            begin_guide(d)
 
     def guide_arrived(d, way):
         from_z = z + d if way == 0 else z - d
@@ -530,16 +537,26 @@
             z * slab + t,
         )
 
-    def text_heads(group, queries, results, first):
+    def text_weights(group, queries, first, slot):
+        def one_head(h, _):
+            at = pl.ds(pl.multiple_of(group * width + h * HDIM, 128), HDIM)
+            q_at = pl.ds(pl.multiple_of(first + h * HDIM, 128), HDIM)
+            k = tk[:, :, :, at].reshape(keys, HDIM)
+            q = queries[:, :, q_at].reshape(slab * rows, HDIM)
+            _, weights, total = weigh(q, k, bias)
+            tp[slot + h] = weights.astype(jnp.bfloat16)
+            tl[slot + h] = total
+            return 0
+
+        lax.fori_loop(0, heads // 2, one_head, 0)
+
+    def text_values(group, results, first, slot):
         def one_head(h, _):
             at = pl.ds(pl.multiple_of(group * width + h * HDIM, 128), HDIM)
             to_at = pl.ds(pl.multiple_of(first + h * HDIM, 128), HDIM)
-            k = tk[:, :, :, at].reshape(keys, HDIM)
             v = tv[:, :, :, at].reshape(keys, HDIM)
-            q = queries[:, :, to_at].reshape(slab * rows, HDIM)
-            _, weights, total = weigh(q, k, bias)
-            out = jnp.dot(weights.astype(jnp.bfloat16), v, preferred_element_type=jnp.float32)
-            out = (out / total).astype(jnp.bfloat16)
+            out = jnp.dot(tp[slot + h], v, preferred_element_type=jnp.float32)
+            out = (out / tl[slot + h]).astype(jnp.bfloat16)
             results[:, :, to_at] = out.reshape(slab, rows, HDIM)
             return 0
 
@@ -549,9 +566,8 @@
     def _():
         for t in range(slab):
             arrived(hq.at[t], hq_recv.at[t])
-        text_heads(0, hq, ho, 0)
-
-    send_if(host, lambda: [repay(t) for t in range(slab)])
+        text_weights(0, hq, 0, heads)
+
     for d in range(1, slabs - 2):
         pass_guide(d)
 
@@ -559,26 +575,18 @@
     def _():
         for j in range(1, slab):
             arrived(half(tq.at[peer(j)], 0), q_recv.at[j, 0])
-        text_heads(0, tq, to, 0)
-
-    send_if(jnp.logical_not(end), lambda: [give(j, 0) for j in others])
+        text_weights(0, tq, 0, 0)
+
     for d in range(slabs - 2, slabs - 1):
         pass_guide(d)
+    begin_chain(1, 0)
+    for j in range(1, slab):
+        arrived(tv.at[z, peer(j)], t_recv.at[j, 1])
+        begin_chain(1, j)
     for j in range(1, slab):
         arrived(half(tq.at[peer(j)], 1), q_recv.at[j, 1])
         arrived(gq.at[peer(j)], q_recv.at[j, 2])
-    text_heads(1, tq, to, width)
-    for j in others:
-        give(j, 1).start()
-    own_att = [
-        pltpu.make_async_copy(half(to.at[s], group), cols(att, s * 2 + group, width), local_sem.at[3 * group])
-        for group in range(2)
-    ]
-    own_att[1].start()
-
-    @pl.when(jnp.logical_not(end))
-    def _():
-        own_att[0].start()
+    text_weights(1, tq, width, heads // 2)
 
     for d in range(1, slabs):
         for way in range(2):
@@ -617,34 +625,35 @@
     for copy in own_part:
         copy.start()
 
+    for d in range(1, slabs):
+        pass_text(d, 1)
+
+    @pl.when(host)
+    def _():
+        text_values(0, ho, 0, heads)
+
+    send_if(host, lambda: [repay(t) for t in range(slab)])
+
+    @pl.when(jnp.logical_not(end))
+    def _():
+        text_values(0, to, 0, 0)
+
+    send_if(jnp.logical_not(end), lambda: [give(j, 0) for j in others])
+    text_values(1, to, width, heads // 2)
+    for j in others:
+        give(j, 1).start()
+    own_att = [
+        pltpu.make_async_copy(half(to.at[s], group), cols(att, s * 2 + group, width), local_sem.at[3 * group])
+        for group in range(2)
+    ]
+    own_att[1].start()
+
+    @pl.when(jnp.logical_not(end))
+    def _():
+        own_att[0].start()
+
     for copy in loads:
         copy.wait()
-    own_att[1].wait()
-    for j in range(1, slab):
-        arrived(cols(att, peer(j) * 2 + 1, width), o_recv.at[j, 1])
-
-    @pl.when(jnp.logical_not(end))
-    def _():
-        own_att[0].wait()
-        for j in range(1, slab):
-            arrived(cols(att, peer(j) * 2, width), o_recv.at[j, 0])
-
-    @pl.when(end)
-    def _():
-        for t in range(slab):
-            arrived(cols(att, t * 2, width), ho_recv.at[t])
-
-    step = 16
-
-    def main_rows(i, _):
-        at = pl.ds(pl.multiple_of(i * step, step), step)
-        summed = v_hidden[at, :].astype(jnp.float32) + att[at, :].astype(jnp.float32)
-        v_shaped[at, :] = shaped_rows(summed, v_mmod[...])
-        return 0
-
-    lax.fori_loop(0, rows // step, main_rows, 0)
-    main_velocity = across(v_mhead[...], v_shaped[...])
-
     for copy in own_part:
         copy.wait()
     for j in range(1, slab):
@@ -670,6 +679,32 @@
     )
     v_gshaped[...] = shaped_rows(guide_sum, v_gmod[...])
     guide_velocity = across(v_ghead[...], v_gshaped[...])
+    own_att[1].wait()
+    for j in range(1, slab):
+        arrived(cols(att, peer(j) * 2 + 1, width), o_recv.at[j, 1])
+
+    @pl.when(jnp.logical_not(end))
+    def _():
+        own_att[0].wait()
+        for j in range(1, slab):
+            arrived(cols(att, peer(j) * 2, width), o_recv.at[j, 0])
+
+    @pl.when(end)
+    def _():
+        for t in range(slab):
+            arrived(cols(att, t * 2, width), ho_recv.at[t])
+
+    step = 16
+
+    def main_rows(i, _):
+        at = pl.ds(pl.multiple_of(i * step, step), step)
+        summed = v_hidden[at, :].astype(jnp.float32) + att[at, :].astype(jnp.float32)
+        v_shaped[at, :] = shaped_rows(summed, v_mmod[...])
+        return 0
+
+    lax.fori_loop(0, rows // step, main_rows, 0)
+    main_velocity = across(v_mhead[...], v_shaped[...])
+
     now = step_index[0]
     plain[...] = guide_velocity
     guided[...] = guidance_scale[0] * (main_velocity - guide_velocity)
@@ -731,6 +766,8 @@
         pltpu.VMEM((rows, width), bf16),
         pltpu.VMEM((slab, rows, text_cols // 2), bf16),
         pltpu.VMEM((slab, rows, text_cols // 2), bf16),
+        pltpu.VMEM((3 * text_cols // 2 // HDIM, slab * rows, slabs * slab * text_rows), bf16),
+        pltpu.VMEM((3 * text_cols // 2 // HDIM, slab * rows, 1), f32),
         pltpu.VMEM((slabs, cores, rows, guide_cols), bf16),
         pltpu.VMEM((slabs, cores, rows, guide_cols), bf16),
         pltpu.VMEM((slab, rows, guide_cols), bf16),

time: 88.9 us -> 77.8 us (0.88)
  Pallas kernels: 84.6 us -> 73.6 us
    pallas_call x1, Pallas kernels: 84.6 us -> 73.6 us  [fused(): pl.pallas_call(functools.partial(kernel, slabs, slab, cores), out_shape=(...]
where the time goes in v4:
time: 77.8 us; the launch traced here: 77.6 us
  Pallas kernels  73.6 us (95%)
  between operations  2.6 us (3%)
  other arithmetic  1.41 us (2%)
    pallas_call x1, Pallas kernels, fused(): pl.pallas_call(functools.partial(kernel, slabs, slab, cores), out_shape=(...  73.6 us

profile of v4, /device:TPU:0, one launch (start us, length us, event | category | flops | bytes accessed | tf_op | source)
XLA Modules:
  0.0 77.6 jit_solution(12006620190911824226)
XLA Ops:
  2.6 0.0 copy-start
  2.6 73.6 %shard_map.185 = (f32[64,96]{1,0:T(8,128)}, f32[64,96]{1,0:T(8,128)}, f32[1,96]{1,0:T(1,128)}) custom-call(s32[1]{0:T(128)S(6)} %copy.20.text_len, f32[1]{0:T(128)S(6)} %copy.21.guidance_scale, f32[51]{0:T(128)} %sigma_table.1, s32[1]{0:T(128)S(6)} %copy.22.step_index, bf16[96,5120]{1,0:T(8,128)(2,1)} %main_hidden.1, bf16[96,5120]{1,0:T(8,128)(2,1)} %main_query.1, ...), custom_call_target="tpu_custom_call" | custom-call | flops 1459617792 | bytes 2621440 | tf_op jit(solution)/shard_map/pallas_call | solution.py:812
  76.2 0.0 copy-done
  76.2 1.4 %fusion = (f32[96,64]{0,1:T(8,128)}, f32[96,64]{0,1:T(8,128)}) fusion(f32[96,64]{0,1:T(8,128)S(1)} %copy-done, f32[96]{0:T(128)} %bitcast.13, f32[64,96]{1,0:T(8,128)} %get-tuple-element.5, f32[64,96]{1,0:T(8,128)} %get-tuple-element.6), kind=kLoop, calls=%fused_computation.1 | loop fusion | flops 18432 | bytes 123264 | tf_op jit(solution)/shard_map/transpose | solution.py:847
Async XLA Ops:
  2.6 73.6 %copy-start = (f32[96,64]{0,1:T(8,128)S(1)}, f32[96,64]{0,1:T(8,128)}, u32[]{:S(2)}) copy-start(f32[96,64]{0,1:T(8,128)} %param.18) | copy-start | bytes 73732

commit v5 on v4

--- a/solution.py
+++ b/solution.py
@@ -406,8 +406,8 @@
     def arrived(place, sem):
         pltpu.make_async_copy(place, place, sem).wait()
 
-    def begin_chain(kv, j):
-        for group in range(2):
+    def begin_chain(kv, j, groups=(0, 1)):
+        for group in groups:
             both_ways(lambda way, group=group: [chain_own(j, kv, group, way)], group)
 
     for j in others:
@@ -421,12 +421,12 @@
         begin_chain(0, j)
     send_if(end, lambda: [lend(t) for t in range(slab)])
     for j in others:
+        slab_text(j, 1).start()
+    for j in others:
         slab_query(j, 1).start()
     send_if(jnp.logical_not(end), lambda: [slab_query(j, 0) for j in others])
     for j in others:
         slab_guide_query(j).start()
-    for j in others:
-        slab_text(j, 1).start()
     for copy in loads:
         copy.start()
     for copy in mine:
@@ -466,11 +466,11 @@
     def coming(d, way):
         return z + d < slabs if way == 0 else z - d >= 0
 
-    def pass_text(d, kv):
+    def pass_text(d, kv, groups=(0, 1)):
         place = both[kv][1]
         for way in range(2):
             from_z = z + d if way == 0 else z - d
-            for group in range(2):
+            for group in groups:
                 comes = coming(d, way)
                 if group == 0:
                     comes = jnp.logical_and(comes, jnp.logical_not(end))
@@ -562,6 +562,11 @@
 
         lax.fori_loop(0, heads // 2, one_head, 0)
 
+    begin_chain(1, 0, (0,))
+    for j in range(1, slab):
+        arrived(tv.at[z, peer(j)], t_recv.at[j, 1])
+        begin_chain(1, j, (0,))
+
     @pl.when(host)
     def _():
         for t in range(slab):
@@ -577,16 +582,32 @@
             arrived(half(tq.at[peer(j)], 0), q_recv.at[j, 0])
         text_weights(0, tq, 0, 0)
 
+    for d in range(1, slabs - 2):
+        pass_text(d, 1, (0,))
     for d in range(slabs - 2, slabs - 1):
         pass_guide(d)
-    begin_chain(1, 0)
-    for j in range(1, slab):
-        arrived(tv.at[z, peer(j)], t_recv.at[j, 1])
-        begin_chain(1, j)
+    for j in range(slab):
+        begin_chain(1, j, (1,))
     for j in range(1, slab):
         arrived(half(tq.at[peer(j)], 1), q_recv.at[j, 1])
         arrived(gq.at[peer(j)], q_recv.at[j, 2])
     text_weights(1, tq, width, heads // 2)
+    for d in range(slabs - 2, slabs):
+        pass_text(d, 1, (0,))
+
+    @pl.when(host)
+    def _():
+        text_values(0, ho, 0, heads)
+
+    send_if(host, lambda: [repay(t) for t in range(slab)])
+
+    @pl.when(jnp.logical_not(end))
+    def _():
+        text_values(0, to, 0, 0)
+
+    send_if(jnp.logical_not(end), lambda: [give(j, 0) for j in others])
+    for d in range(1, slabs - 2):
+        pass_text(d, 1, (1,))
 
     for d in range(1, slabs):
         for way in range(2):
@@ -604,7 +625,7 @@
         v = gv[:, :, :, at].reshape(guide_keys, HDIM)
         peak, weights, total = weigh(gq[:, :, at].reshape(slab * rows, HDIM), k)
         out = jnp.dot(weights.astype(jnp.bfloat16), v, preferred_element_type=jnp.float32)
-        gacc[:, :, at] = out.reshape(slab, rows, HDIM)
+        gacc[:, :, at] = (out / total).astype(jnp.bfloat16).reshape(slab, rows, HDIM)
         gml[:, :, h : h + 1] = peak.reshape(slab, rows, 1)
         gml[:, :, guide_heads + h : guide_heads + h + 1] = total.reshape(slab, rows, 1)
 
@@ -625,20 +646,8 @@
     for copy in own_part:
         copy.start()
 
-    for d in range(1, slabs):
-        pass_text(d, 1)
-
-    @pl.when(host)
-    def _():
-        text_values(0, ho, 0, heads)
-
-    send_if(host, lambda: [repay(t) for t in range(slab)])
-
-    @pl.when(jnp.logical_not(end))
-    def _():
-        text_values(0, to, 0, 0)
-
-    send_if(jnp.logical_not(end), lambda: [give(j, 0) for j in others])
+    for d in range(slabs - 2, slabs):
+        pass_text(d, 1, (1,))
     text_values(1, to, width, heads // 2)
     for j in others:
         give(j, 1).start()
@@ -667,10 +676,10 @@
             peaks = [rml[t, :, h : h + 1] for t in members]
             totals = [rml[t, :, guide_heads + h : guide_heads + h + 1] for t in members]
             peak = functools.reduce(jnp.maximum, peaks)
-            factors = [jnp.exp2((p - peak) * scale) for p in peaks]
-            total = sum(f * l for f, l in zip(factors, totals))
+            factors = [l * jnp.exp2((p - peak) * scale) for p, l in zip(peaks, totals)]
+            total = sum(factors)
             summed = sum(
-                f * racc[t, :, h * HDIM : (h + 1) * HDIM] for f, t in zip(factors, members)
+                f * racc[t, :, h * HDIM : (h + 1) * HDIM].astype(jnp.float32) for f, t in zip(factors, members)
             )
             pieces.append((summed / total).astype(jnp.bfloat16))
     guide_attended = jnp.concatenate(pieces, axis=-1)
@@ -771,9 +780,9 @@
         pltpu.VMEM((slabs, cores, rows, guide_cols), bf16),
         pltpu.VMEM((slabs, cores, rows, guide_cols), bf16),
         pltpu.VMEM((slab, rows, guide_cols), bf16),
-        pltpu.VMEM((slab, rows, guide_cols), f32),
+        pltpu.VMEM((slab, rows, guide_cols), bf16),
         pltpu.VMEM((slab, rows, 128), f32),
-        pltpu.VMEM((slab, rows, guide_cols), f32),
+        pltpu.VMEM((slab, rows, guide_cols), bf16),
         pltpu.VMEM((slab, rows, 128), f32),
         like(main_hidden),
         like(guide_hidden),

time: 77.8 us -> 83.6 us (1.075)
  Pallas kernels: 73.6 us -> 79.3 us
    pallas_call x1, Pallas kernels: 73.6 us -> 79.3 us  [fused(): pl.pallas_call(functools.partial(kernel, slabs, slab, cores), out_shape=(...]
where the time goes in v5:
time: 83.6 us; the launch traced here: 83.3 us
  Pallas kernels  79.3 us (95%)
  between operations  2.6 us (3%)
  other arithmetic  1.41 us (2%)
    pallas_call x1, Pallas kernels, fused(): pl.pallas_call(functools.partial(kernel, slabs, slab, cores), out_shape=(...  79.3 us

profile of v5, /device:TPU:0, one launch (start us, length us, event | category | flops | bytes accessed | tf_op | source)
XLA Modules:
  0.0 83.3 jit_solution(5572906531417092960)
XLA Ops:
  2.6 0.0 copy-start
  2.6 79.3 %shard_map.185 = (f32[64,96]{1,0:T(8,128)}, f32[64,96]{1,0:T(8,128)}, f32[1,96]{1,0:T(1,128)}) custom-call(s32[1]{0:T(128)S(6)} %copy.20.text_len, f32[1]{0:T(128)S(6)} %copy.21.guidance_scale, f32[51]{0:T(128)} %sigma_table.1, s32[1]{0:T(128)S(6)} %copy.22.step_index, bf16[96,5120]{1,0:T(8,128)(2,1)} %main_hidden.1, bf16[96,5120]{1,0:T(8,128)(2,1)} %main_query.1, ...), custom_call_target="tpu_custom_call" | custom-call | flops 1459617792 | bytes 2621440 | tf_op jit(solution)/shard_map/pallas_call | solution.py:821
  81.9 0.0 copy-done
  81.9 1.4 %fusion = (f32[96,64]{0,1:T(8,128)}, f32[96,64]{0,1:T(8,128)}) fusion(f32[96,64]{0,1:T(8,128)S(1)} %copy-done, f32[96]{0:T(128)} %bitcast.13, f32[64,96]{1,0:T(8,128)} %get-tuple-element.5, f32[64,96]{1,0:T(8,128)} %get-tuple-element.6), kind=kLoop, calls=%fused_computation.1 | loop fusion | flops 18432 | bytes 123264 | tf_op jit(solution)/shard_map/transpose | solution.py:856
Async XLA Ops:
  2.6 79.3 %copy-start = (f32[96,64]{0,1:T(8,128)S(1)}, f32[96,64]{0,1:T(8,128)}, u32[]{:S(2)}) copy-start(f32[96,64]{0,1:T(8,128)} %param.18) | copy-start | bytes 73732

commit v6 on v5

--- a/solution.py
+++ b/solution.py
@@ -575,6 +575,8 @@
 
     for d in range(1, slabs - 2):
         pass_guide(d)
+    for j in range(slab):
+        begin_chain(1, j, (1,))
 
     @pl.when(jnp.logical_not(end))
     def _():
@@ -583,32 +585,13 @@
         text_weights(0, tq, 0, 0)
 
     for d in range(1, slabs - 2):
-        pass_text(d, 1, (0,))
+        pass_text(d, 1)
     for d in range(slabs - 2, slabs - 1):
         pass_guide(d)
-    for j in range(slab):
-        begin_chain(1, j, (1,))
     for j in range(1, slab):
         arrived(half(tq.at[peer(j)], 1), q_recv.at[j, 1])
         arrived(gq.at[peer(j)], q_recv.at[j, 2])
     text_weights(1, tq, width, heads // 2)
-    for d in range(slabs - 2, slabs):
-        pass_text(d, 1, (0,))
-
-    @pl.when(host)
-    def _():
-        text_values(0, ho, 0, heads)
-
-    send_if(host, lambda: [repay(t) for t in range(slab)])
-
-    @pl.when(jnp.logical_not(end))
-    def _():
-        text_values(0, to, 0, 0)
-
-    send_if(jnp.logical_not(end), lambda: [give(j, 0) for j in others])
-    for d in range(1, slabs - 2):
-        pass_text(d, 1, (1,))
-
     for d in range(1, slabs):
         for way in range(2):
             comes = z + d < slabs if way == 0 else z - d >= 0
@@ -646,8 +629,20 @@
     for copy in own_part:
         copy.start()
 
-    for d in range(slabs - 2, slabs):
-        pass_text(d, 1, (1,))
+    pass_text(slabs - 2, 1)
+
+    @pl.when(host)
+    def _():
+        text_values(0, ho, 0, heads)
+
+    send_if(host, lambda: [repay(t) for t in range(slab)])
+
+    @pl.when(jnp.logical_not(end))
+    def _():
+        text_values(0, to, 0, 0)
+
+    send_if(jnp.logical_not(end), lambda: [give(j, 0) for j in others])
+    pass_text(slabs - 1, 1)
     text_values(1, to, width, heads // 2)
     for j in others:
         give(j, 1).start()

time: 83.6 us -> 79.9 us (0.956)
  Pallas kernels: 79.3 us -> 75.6 us
    pallas_call x1, Pallas kernels: 79.3 us -> 75.6 us  [fused(): pl.pallas_call(functools.partial(kernel, slabs, slab, cores), out_shape=(...]
where the time goes in v6:
time: 79.9 us; the launch traced here: 79.6 us
  Pallas kernels  75.6 us (95%)
  between operations  2.6 us (3%)
  other arithmetic  1.41 us (2%)
    pallas_call x1, Pallas kernels, fused(): pl.pallas_call(functools.partial(kernel, slabs, slab, cores), out_shape=(...  75.6 us

profile of v6, /device:TPU:0, one launch (start us, length us, event | category | flops | bytes accessed | tf_op | source)
XLA Modules:
  0.0 79.6 jit_solution(8384259904541987653)
XLA Ops:
  2.6 0.0 copy-start
  2.6 75.6 %shard_map.185 = (f32[64,96]{1,0:T(8,128)}, f32[64,96]{1,0:T(8,128)}, f32[1,96]{1,0:T(1,128)}) custom-call(s32[1]{0:T(128)S(6)} %copy.20.text_len, f32[1]{0:T(128)S(6)} %copy.21.guidance_scale, f32[51]{0:T(128)} %sigma_table.1, s32[1]{0:T(128)S(6)} %copy.22.step_index, bf16[96,5120]{1,0:T(8,128)(2,1)} %main_hidden.1, bf16[96,5120]{1,0:T(8,128)(2,1)} %main_query.1, ...), custom_call_target="tpu_custom_call" | custom-call | flops 1459617792 | bytes 2621440 | tf_op jit(solution)/shard_map/pallas_call | solution.py:816
  78.2 0.0 copy-done
  78.2 1.4 %fusion = (f32[96,64]{0,1:T(8,128)}, f32[96,64]{0,1:T(8,128)}) fusion(f32[96,64]{0,1:T(8,128)S(1)} %copy-done, f32[96]{0:T(128)} %bitcast.13, f32[64,96]{1,0:T(8,128)} %get-tuple-element.5, f32[64,96]{1,0:T(8,128)} %get-tuple-element.6), kind=kLoop, calls=%fused_computation.1 | loop fusion | flops 18432 | bytes 123264 | tf_op jit(solution)/shard_map/transpose | solution.py:851
Async XLA Ops:
  2.6 75.6 %copy-start = (f32[96,64]{0,1:T(8,128)S(1)}, f32[96,64]{0,1:T(8,128)}, u32[]{:S(2)}) copy-start(f32[96,64]{0,1:T(8,128)} %param.18) | copy-start | bytes 73732

commit v7 on v4

--- a/solution.py
+++ b/solution.py
@@ -577,12 +577,12 @@
             arrived(half(tq.at[peer(j)], 0), q_recv.at[j, 0])
         text_weights(0, tq, 0, 0)
 
-    for d in range(slabs - 2, slabs - 1):
-        pass_guide(d)
     begin_chain(1, 0)
     for j in range(1, slab):
         arrived(tv.at[z, peer(j)], t_recv.at[j, 1])
         begin_chain(1, j)
+    for d in range(slabs - 2, slabs - 1):
+        pass_guide(d)
     for j in range(1, slab):
         arrived(half(tq.at[peer(j)], 1), q_recv.at[j, 1])
         arrived(gq.at[peer(j)], q_recv.at[j, 2])
@@ -604,7 +604,7 @@
         v = gv[:, :, :, at].reshape(guide_keys, HDIM)
         peak, weights, total = weigh(gq[:, :, at].reshape(slab * rows, HDIM), k)
         out = jnp.dot(weights.astype(jnp.bfloat16), v, preferred_element_type=jnp.float32)
-        gacc[:, :, at] = out.reshape(slab, rows, HDIM)
+        gacc[:, :, at] = (out / total).astype(jnp.bfloat16).reshape(slab, rows, HDIM)
         gml[:, :, h : h + 1] = peak.reshape(slab, rows, 1)
         gml[:, :, guide_heads + h : guide_heads + h + 1] = total.reshape(slab, rows, 1)
 
@@ -667,10 +667,10 @@
             peaks = [rml[t, :, h : h + 1] for t in members]
             totals = [rml[t, :, guide_heads + h : guide_heads + h + 1] for t in members]
             peak = functools.reduce(jnp.maximum, peaks)
-            factors = [jnp.exp2((p - peak) * scale) for p in peaks]
-            total = sum(f * l for f, l in zip(factors, totals))
+            factors = [l * jnp.exp2((p - peak) * scale) for p, l in zip(peaks, totals)]
+            total = sum(factors)
             summed = sum(
-                f * racc[t, :, h * HDIM : (h + 1) * HDIM] for f, t in zip(factors, members)
+                f * racc[t, :, h * HDIM : (h + 1) * HDIM].astype(jnp.float32) for f, t in zip(factors, members)
             )
             pieces.append((summed / total).astype(jnp.bfloat16))
     guide_attended = jnp.concatenate(pieces, axis=-1)
@@ -771,9 +771,9 @@
         pltpu.VMEM((slabs, cores, rows, guide_cols), bf16),
         pltpu.VMEM((slabs, cores, rows, guide_cols), bf16),
         pltpu.VMEM((slab, rows, guide_cols), bf16),
-        pltpu.VMEM((slab, rows, guide_cols), f32),
+        pltpu.VMEM((slab, rows, guide_cols), bf16),
         pltpu.VMEM((slab, rows, 128), f32),
-        pltpu.VMEM((slab, rows, guide_cols), f32),
+        pltpu.VMEM((slab, rows, guide_cols), bf16),
         pltpu.VMEM((slab, rows, 128), f32),
         like(main_hidden),
         like(guide_hidden),

time: 77.8 us -> 78.6 us (1.010)
  no operation moved by 1% of the time
where the time goes in v7:
time: 78.6 us; the launch traced here: 78.3 us
  Pallas kernels  74.3 us (95%)
  between operations  2.6 us (3%)
  other arithmetic  1.41 us (2%)
    pallas_call x1, Pallas kernels, fused(): pl.pallas_call(functools.partial(kernel, slabs, slab, cores), out_shape=(...  74.3 us

profile of v7, /device:TPU:0, one launch (start us, length us, event | category | flops | bytes accessed | tf_op | source)
XLA Modules:
  0.0 78.3 jit_solution(11278075650735768868)
XLA Ops:
  2.6 0.0 copy-start
  2.6 74.3 %shard_map.185 = (f32[64,96]{1,0:T(8,128)}, f32[64,96]{1,0:T(8,128)}, f32[1,96]{1,0:T(1,128)}) custom-call(s32[1]{0:T(128)S(6)} %copy.20.text_len, f32[1]{0:T(128)S(6)} %copy.21.guidance_scale, f32[51]{0:T(128)} %sigma_table.1, s32[1]{0:T(128)S(6)} %copy.22.step_index, bf16[96,5120]{1,0:T(8,128)(2,1)} %main_hidden.1, bf16[96,5120]{1,0:T(8,128)(2,1)} %main_query.1, ...), custom_call_target="tpu_custom_call" | custom-call | flops 1459617792 | bytes 2621440 | tf_op jit(solution)/shard_map/pallas_call | solution.py:812
  76.9 0.0 copy-done
  76.9 1.4 %fusion = (f32[96,64]{0,1:T(8,128)}, f32[96,64]{0,1:T(8,128)}) fusion(f32[96,64]{0,1:T(8,128)S(1)} %copy-done, f32[96]{0:T(128)} %bitcast.13, f32[64,96]{1,0:T(8,128)} %get-tuple-element.5, f32[64,96]{1,0:T(8,128)} %get-tuple-element.6), kind=kLoop, calls=%fused_computation.1 | loop fusion | flops 18432 | bytes 123264 | tf_op jit(solution)/shard_map/transpose | solution.py:847
Async XLA Ops:
  2.6 74.3 %copy-start = (f32[96,64]{0,1:T(8,128)S(1)}, f32[96,64]{0,1:T(8,128)}, u32[]{:S(2)}) copy-start(f32[96,64]{0,1:T(8,128)} %param.18) | copy-start | bytes 73732
